TPU v7x, 32 devices: a whole 2x2x4 slice. The times are simulated.
32 devices in a mesh: fsdp: 2 (over x), dp: 16 (over z, y, core).
Axes of the slice: x: 2, y: 2, z: 4, core: 2. Of those that a mesh axis runs over, the one named last changes fastest.
Arguments:
- tokens: bfloat16 [2, 16, 1024, 768], P('fsdp', 'dp'), may hold values from -6 to 6
- live: int32 [2, 16], P('fsdp', 'dp'), may hold values from 0 to 1, as said below
- norm_gain: bfloat16 [768], P('fsdp'), may hold values from 0.5 to 1.5
- w_in: bfloat16 [768, 3352], P('fsdp'), may hold values from -0.21875 to 0.21875
- conv_weight: bfloat16 [1792, 4], P('fsdp'), may hold values from -3 to 3
- conv_bias: bfloat16 [1792], P('fsdp'), may hold values from -3 to 3
- dt_bias: bfloat16 [24], P('fsdp'), may hold values from -4 to 0
- a_log: bfloat16 [24], P('fsdp'), may hold values from -3 to 1
- d_skip: bfloat16 [24], P('fsdp'), may hold values from 0.5 to 1.5
- inner_gain: bfloat16 [1536], P('fsdp'), may hold values from 0.5 to 1.5
- w_out: bfloat16 [1536, 768], P('fsdp'), may hold values from -0.15625 to 0.15625
- cotangent: bfloat16 [2, 16, 1024, 768], P('fsdp', 'dp'), may hold values from -6 to 6
Outputs:
- block_out: bfloat16 [2, 16, 1024, 768], P('fsdp', 'dp')
- input_grad: float32 [2, 16, 1024, 768], P('fsdp', 'dp')
- norm_gain_grad: float32 [768], P('fsdp')
- w_in_grad: float32 [768, 3352], P('fsdp')
- conv_weight_grad: float32 [1792, 4], P('fsdp')
- conv_bias_grad: float32 [1792], P('fsdp')
- dt_bias_grad: float32 [24], P('fsdp')
- a_log_grad: float32 [24], P('fsdp')
- d_skip_grad: float32 [24], P('fsdp')
- inner_gain_grad: float32 [1536], P('fsdp')
- w_out_grad: float32 [1536, 768], P('fsdp')
Inputs may be any that keep to these rules, and one draw needn't show every extreme that they name: `live`: 1 marks a device that holds a sequence; some devices hold none.
All inputs are finite; a program needn't handle non-finite values.
Results may differ from a plain program's by a relative error of at most 0.0097.
Values may be sent and summed in bfloat16 or wider, within the bound.
No kernel may reach another device: no remote copies, remote signals or barrier semaphores. Data moves between devices by JAX's collectives and lax.ppermute only.
A program may use at most 192 MiB of HBM per device.

v0:
```python
import jax
import jax.numpy as jnp
from jax import lax
from jax.sharding import PartitionSpec as P

STRETCH = 256


EPSILON = 1e-05
PRECISE = lax.Precision.HIGHEST


def normalize(seq_input, norm_gain):
    return (
        seq_input
        * lax.rsqrt(jnp.mean(seq_input * seq_input, axis=1, keepdims=True) + EPSILON)
        * norm_gain[None, :]
    )


def convolve_inputs(mixed_in, raw_step, conv_weight, conv_bias, dt_bias):
    length = mixed_in.shape[0]
    taps = conv_weight.shape[1]
    padded = jnp.pad(mixed_in, ((taps - 1, 0), (0, 0)))
    summed = conv_bias[None, :] + padded[0:length] * conv_weight[:, 0][None, :]
    for offset in range(1, taps):
        summed = summed + padded[offset : offset + length] * conv_weight[:, offset][None, :]
    activated = jax.nn.silu(summed)
    step_size = jax.nn.softplus(raw_step + dt_bias[None, :])
    return (activated, step_size)


def block_update(state, value_block, b_block, c_block, step_block, rates, d_skip):
    span = value_block.shape[0]
    heads = value_block.shape[1]
    head_dim = value_block.shape[2]
    cumulated = jnp.cumsum(step_block * rates[None, :], axis=0).T
    scores = jnp.dot(c_block, b_block.T, precision=PRECISE)
    row_index = lax.broadcasted_iota(jnp.int32, (span, span), 0)
    col_index = lax.broadcasted_iota(jnp.int32, (span, span), 1)
    causal = (row_index >= col_index)[None, :, :]
    gaps = jnp.where(causal, cumulated[:, :, None] - cumulated[:, None, :], 0.0)
    decay_factor = jnp.where(causal, jnp.exp(gaps), 0.0)
    weights = scores[None, :, :] * decay_factor * step_block.T[:, None, :]
    intra_part = jnp.einsum("hts,shp->thp", weights, value_block, precision=PRECISE)
    carried = jnp.exp(cumulated).T[:, :, None] * jnp.einsum(
        "hpn,tn->thp", state, c_block, precision=PRECISE
    )
    stretch_total = cumulated[:, -1]
    factor = jnp.exp(stretch_total[:, None] - cumulated) * step_block.T
    scaled = value_block * factor.T[:, :, None]
    new_state = jnp.exp(stretch_total)[:, None, None] * state + jnp.einsum(
        "shp,sn->hpn", scaled, b_block, precision=PRECISE
    )
    result = intra_part + carried + d_skip[None, :, None] * value_block
    return (new_state, result.reshape(span, heads * head_dim))


def stretch_recurrence(values, inputs_b, inputs_c, step_size, a_log, d_skip):
    length = values.shape[0]
    heads = values.shape[1]
    head_dim = values.shape[2]
    state_dim = inputs_b.shape[1]
    blocks = length // STRETCH
    rates = -jnp.exp(a_log)
    update = jax.checkpoint(block_update)
    state = jnp.zeros((heads, head_dim, state_dim), jnp.float32)
    pieces = []
    for block in range(blocks):
        first = block * STRETCH
        state, piece = update(
            state,
            values[first : first + STRETCH],
            inputs_b[first : first + STRETCH],
            inputs_c[first : first + STRETCH],
            step_size[first : first + STRETCH],
            rates,
            d_skip,
        )
        pieces.append(piece)
    return jnp.concatenate(pieces, axis=0)


def state_scan(rounded, step_size, gate_part, a_log, d_skip, inner_gain):
    length = rounded.shape[0]
    heads = a_log.shape[0]
    inner_width = inner_gain.shape[0]
    state_dim = (rounded.shape[1] - inner_width) // 2
    values = rounded[:, :inner_width].reshape(length, heads, inner_width // heads)
    scanned = stretch_recurrence(
        values,
        rounded[:, inner_width : inner_width + state_dim],
        rounded[:, inner_width + state_dim :],
        step_size,
        a_log,
        d_skip,
    )
    gated = scanned * jax.nn.silu(gate_part)
    return (
        gated
        * lax.rsqrt(jnp.mean(gated * gated, axis=1, keepdims=True) + EPSILON)
        * inner_gain[None, :]
    )


def take_share(total, owner_index, groups):
    rows_each = total.shape[0] // groups
    return lax.dynamic_slice_in_dim(total, owner_index * rows_each, rows_each, 0)


def shards(
    tokens,
    live,
    norm_gain,
    w_in,
    conv_weight,
    conv_bias,
    dt_bias,
    a_log,
    d_skip,
    inner_gain,
    w_out,
    cotangent,
):
    gathered = (
        lax.all_gather(norm_gain, "fsdp", axis=0, tiled=True),
        lax.all_gather(w_in, "fsdp", axis=0, tiled=True),
        lax.all_gather(conv_weight, "fsdp", axis=0, tiled=True),
        lax.all_gather(conv_bias, "fsdp", axis=0, tiled=True),
        lax.all_gather(dt_bias, "fsdp", axis=0, tiled=True),
        lax.all_gather(a_log, "fsdp", axis=0, tiled=True),
        lax.all_gather(d_skip, "fsdp", axis=0, tiled=True),
        lax.all_gather(inner_gain, "fsdp", axis=0, tiled=True),
        lax.all_gather(w_out, "fsdp", axis=0, tiled=True),
    )
    (
        gain_all,
        proj_weight,
        conv_all,
        shift_all,
        step_bias,
        log_rate,
        skip_all,
        inner_all,
        out_weight,
    ) = gathered
    gain_float = gain_all.astype(jnp.float32)
    conv_float = conv_all.astype(jnp.float32)
    shift_float = shift_all.astype(jnp.float32)
    bias_float = step_bias.astype(jnp.float32)
    rate_float = log_rate.astype(jnp.float32)
    skip_float = skip_all.astype(jnp.float32)
    inner_float = inner_all.astype(jnp.float32)
    inner_width = out_weight.shape[0]
    conv_width = conv_all.shape[0]
    alive = live[0, 0].astype(jnp.float32)
    seq_input = tokens[0, 0].astype(jnp.float32)
    normed, pull_norm = jax.vjp(normalize, seq_input, gain_float)
    low_normed = normed.astype(jnp.bfloat16)
    projected = jnp.dot(low_normed, proj_weight, preferred_element_type=jnp.float32)
    gate_part = projected[:, :inner_width]
    mixed_in = projected[:, inner_width : inner_width + conv_width]
    raw_step = projected[:, inner_width + conv_width :]
    (activated, step_size), pull_mix = jax.vjp(
        convolve_inputs, mixed_in, raw_step, conv_float, shift_float, bias_float
    )
    rounded = lax.optimization_barrier(activated.astype(jnp.bfloat16)).astype(jnp.float32)
    mixed_out, pull_scan = jax.vjp(
        state_scan, rounded, step_size, gate_part, rate_float, skip_float, inner_float
    )
    low_mixed = mixed_out.astype(jnp.bfloat16)
    branch = jnp.dot(low_mixed, out_weight, preferred_element_type=jnp.float32)
    block_out = (alive * (seq_input + branch)).astype(jnp.bfloat16).reshape(tokens.shape)
    incoming = (cotangent[0, 0].astype(jnp.float32) * alive).astype(jnp.bfloat16)
    contract_last = (((1,), (1,)), ((), ()))
    contract_first = (((0,), (0,)), ((), ()))
    d_mixed = lax.dot_general(
        incoming, out_weight, contract_last, preferred_element_type=jnp.float32
    )
    d_out_weight = lax.dot_general(
        low_mixed, incoming, contract_first, preferred_element_type=jnp.float32
    )
    d_rounded, d_step, d_gate, d_rate, d_skip_term, d_inner = pull_scan(d_mixed)
    d_mixed_in, d_raw, d_conv, d_shift, d_bias = pull_mix((d_rounded, d_step))
    d_projected = jnp.concatenate([d_gate, d_mixed_in, d_raw], axis=1).astype(jnp.bfloat16)
    d_normed = lax.dot_general(
        d_projected, proj_weight, contract_last, preferred_element_type=jnp.float32
    )
    d_proj_weight = lax.dot_general(
        low_normed, d_projected, contract_first, preferred_element_type=jnp.float32
    )
    d_seq, d_gain = pull_norm(d_normed)
    input_grad = (incoming.astype(jnp.float32) + d_seq).reshape(cotangent.shape)
    totals = lax.psum(
        (
            d_gain,
            d_proj_weight,
            d_conv,
            d_shift,
            d_bias,
            d_rate,
            d_skip_term,
            d_inner,
            d_out_weight,
        ),
        ("fsdp", "dp"),
    )
    owner_index = lax.axis_index("fsdp")
    groups = lax.axis_size("fsdp")
    g_gain, g_proj, g_conv, g_shift, g_bias, g_rate, g_skip, g_inner, g_out = [
        take_share(total, owner_index, groups) for total in totals
    ]
    return (
        block_out,
        input_grad,
        g_gain,
        g_proj,
        g_conv,
        g_shift,
        g_bias,
        g_rate,
        g_skip,
        g_inner,
        g_out,
    )


def solution(mesh):
    placed = (
        P("fsdp", "dp", None, None),
        P("fsdp", "dp"),
        P("fsdp"),
        P("fsdp", None),
        P("fsdp", None),
        P("fsdp"),
        P("fsdp"),
        P("fsdp"),
        P("fsdp"),
        P("fsdp"),
        P("fsdp", None),
        P("fsdp", "dp", None, None),
    )
    return jax.shard_map(
        shards,
        mesh=mesh,
        in_specs=placed,
        out_specs=(
            P("fsdp", "dp", None, None),
            P("fsdp", "dp", None, None),
            P("fsdp"),
            P("fsdp", None),
            P("fsdp", None),
            P("fsdp"),
            P("fsdp"),
            P("fsdp"),
            P("fsdp"),
            P("fsdp"),
            P("fsdp", None),
        ),
        check_vma=False,
    )
```

profile of v0, /device:TPU:1, one launch (start us, length us, event | category | flops | bytes accessed | tf_op | source)
XLA Modules:
  0.0 827.8 jit_solution(13320768039607271562)
XLA Ops:
  12.1 4.3 all-reduce.36
  17.1 3.2 all-gather.1
  20.3 3.2 all-gather.2
  23.6 3.9 all-gather
  27.9 3.7 all_gather.30
  31.8 47.8 %all-gather.6.cloned.1.call-done = bf16[768,3352]{0,1:T(8,128)(2,1)} async-done(((bf16[384,3352]{0,1:T(8,128)(2,1)}), bf16[768,3352]{0,1:T(8,128)(2,1)}) %all-gather.6.cloned.1.call-update) | async-done | bytes 5148688 | tf_op jit(solution)/shard_map/all_gather | solution.py:127
  79.5 7.7 fusion.230
  87.3 5.5 copy-done.2
  104.4 3.8 slice.322
  108.3 9.4 %multiply_convert_fusion = (bf16[1024,1792]{0,1:T(8,128)(2,1)S(1)}, f32[1024,1792]{0,1:T(8,128)}) fusion(f32[1024,1792]{0,1:T(8,128)S(1)} %slice.322, f32[1792]{0:T(1024)S(1)} %get-tuple-element.125, f32[1792]{0:T(1024)S(1)} %get-tuple-element.126, f32[1792]{0:T(1024)S(1)} %get-tuple-element.127, f32[1792]{0:T(1024)S(1)} %get-tuple-element.124, ...), kind=kLoop, calls=%fused_computation.16 | loop fusion | flops 23855104 | bytes 18385920 | tf_op jit(solution)/shard_map/convert_element_type | solution.py:167
  145.5 2.3 fusion.179
  157.0 5.3 fusion.129
  162.4 5.1 fusion.128
  167.6 5.1 fusion.127
  172.7 5.5 fusion.126
  178.2 5.1 multiply_reduce_fusion.14
  183.4 2.9 fusion.328
  186.3 4.6 fusion.188
  190.9 8.1 multiply_reduce_fusion.4
  199.1 7.7 fusion.5
  216.6 3.7 multiply_reduce_fusion.25
  220.3 3.3 fusion.192
  223.6 2.3 fusion.169
  236.8 2.4 multiply_reduce_fusion.28
  239.2 3.2 multiply_reduce_fusion.23
  243.5 3.4 multiply_reduce_fusion.17
  252.1 3.3 fusion.195
  255.4 3.6 fusion.173
  271.8 2.4 multiply_reduce_fusion.27
  274.2 3.2 multiply_reduce_fusion.21
  278.6 3.4 multiply_reduce_fusion.16
  287.1 3.3 fusion.198
  290.4 3.5 fusion.176
  296.2 2.3 reduce-window.104
  316.3 2.2 multiply_reduce_fusion.26
  318.5 3.5 multiply_reduce_fusion.19
  325.6 5.4 multiply_reduce_fusion.15
  332.5 2.3 multiply_bitcast_fusion
  336.4 3.8 fusion.210
  341.8 3.1 fusion.201
  344.9 7.4 fusion.334
  352.3 5.2 fusion.333
  357.6 5.2 fusion.332
  362.9 7.0 bitcast_add_fusion.3
  370.1 22.3 %fusion.59 = (f32[24,256]{1,0:T(8,128)S(1)}, f32[24,256]{1,0:T(8,128)S(1)}, f32[24,256]{1,0:T(8,128)}, f32[256,256]{1,0:T(8,128)S(1)}, f32[256,256]{1,0:T(8,128)...) fusion(f32[256,256]{1,0:T(8,128)S(1)} %copy-done.79, ...), kind=kOutput, calls=%fused_computation.105 | convolution fusion | flops 1301995520 | bytes 24674304 | tf_op jit(solution)/shard_map/transpose(jvp(jvp()))/checkpoint/hts,shp->thp/dot_general | solution.py:45
  397.1 3.8 reduce-window.106
  416.1 3.1 fusion.204
  424.8 4.2 reduce-window.110
  442.6 3.8 reduce-window.116
  460.1 3.1 fusion.207
  468.9 3.8 reduce-window.114
  484.4 8.4 %bitcast_add_fusion = f32[256,24,64]{0,2,1:T(8,128)S(1)} fusion(f32[256,24,64]{0,2,1:T(8,128)} %get-tuple-element.217, f32[256,24,64]{0,2,1:T(8,128)} %bitcast.528, f32[24,64,256]{2,1,0:T(8,128)} %bitcast.527, f32[256,256]{1,0:T(8,128)} %fusion.339, f32[24,256]{1,0:T(8,128)} %copy.365, f32[24,256]{1,0:T(8,128)} %copy.364, ...), kind=kOutput, calls=%fused_computation.173 | convolution fusion | flops 1217396736 | bytes 6692960 | tf_op jit(solution)/shard_map/transpose(jvp(jvp()))/checkpoint/hts,shp->thp/dot_general | solution.py:45
  493.0 5.7 bitcast_add_fusion.2
  498.8 5.7 bitcast_add_fusion.1
  507.9 12.1 %multiply_reduce_fusion.2 = (f32[1792]{0:T(1024)S(1)}, f32[1792]{0:T(1024)S(1)}, f32[1792]{0:T(1024)S(1)}, f32[1792]{0:T(1024)S(1)}, f32[1792]{0:T(1024)S(1)}, /*index=5*/f32[1024,1792]{0,1:T(8,128)S(1)}) fusion(f32[1024,1792]{0,1:T(8,128)S(1)} %bitcast.496, f32[1024,3352]{0,1:T(8,128)} %copy-done.2, f32[1024,1792]{0,1:T(8,128)S(1)} %bitcast.540, ...), kind=kLoop, calls=%fused_computation.14 | loop fusion | flops 36691200 | bytes 36736000 | tf_op jit(solution)/shard_map/transpose(jvp())/reduce_sum | solution.py:27
  520.1 8.5 %broadcast_multiply_fusion = (f32[1024,1792]{0,1:T(8,128)S(1)}, f32[1024,1792]{0,1:T(8,128)}, f32[1024,1792]{0,1:T(8,128)}, f32[1024,1792]{0,1:T(8,128)}) fusion(f32[1024,1792]{0,1:T(8,128)S(1)} %get-tuple-element.142, f32[1792]{0:T(1024)S(1)} %copy-done.88, f32[1792]{0:T(1024)S(1)} %copy-done.86, f32[1792]{0:T(1024)S(1)} %copy-done.92, f32[1792]{0:T(1024)S(1)} %copy-done.90), kind=kLoop, calls=%fused_computation.100 | loop fusion | flops 7340032 | bytes 36728832 | tf_op jit(solution)/shard_map/transpose(jvp())/mul | solution.py:27
  528.6 12.0 %fusion.2 = bf16[1024,1792]{0,1:T(8,128)(2,1)} fusion(f32[1024,1792]{0,1:T(8,128)} %get-tuple-element.150, f32[1024,1792]{0,1:T(8,128)} %get-tuple-element.151, f32[1024,1792]{0,1:T(8,128)} %get-tuple-element.152, f32[1024,1792]{0,1:T(8,128)S(1)} %get-tuple-element.149), kind=kLoop, calls=%fused_computation.9 | loop fusion | flops 7340032 | bytes 33030144 | tf_op jit(solution)/shard_map/convert.4
  540.6 12.5 %fusion.123 = f32[768,3352]{0,1:T(8,128)} fusion(bf16[1024,24]{0,1:T(8,128)(2,1)S(1)} %copy.410, bf16[1024,1792]{0,1:T(8,128)(2,1)} %fusion.2, bf16[1024,1536]{0,1:T(8,128)(2,1)} %get-tuple-element.147, bf16[1,1,1024,768]{3,2,1,0:T(8,128)(2,1)S(1)} %copy-done.22, f32[768]{0:T(1024)S(1)} %copy-done.125, f32[1024]{0:T(1024)S(1)} %copy-done.127), kind=kOutput, calls=%fused_computation.170 | convolution fusion | flops 5295980544 | bytes 18742272 | tf_op jit(solution)/shard_map/dot_general | solution.py:189
  556.3 12.4 %fusion.67 = (f32[768]{0:T(1024)S(1)}, f32[1024]{0:T(1024)S(1)}, f32[1024,768]{1,0:T(8,128)}) fusion(bf16[1,1,1024,768]{3,2,1,0:T(8,128)(2,1)S(1)} %copy-done.22, f32[1024]{0:T(1024)S(1)} %copy-done.127, f32[768]{0:T(1024)S(1)} %copy-done.125, bf16[768,3352]{0,1:T(8,128)(2,1)} %all-gather.6.cloned.1.call-done, bf16[1024,24]{0,1:T(8,128)(2,1)S(1)} %copy.410, ...), kind=kOutput, calls=%fused_computation.113 | convolution fusion | flops 5298337792 | bytes 16746496 | tf_op jit(solution)/shard_map/dot_general | solution.py:186
  568.7 41.9 %all-reduce.34 = (f32[768]{0:T(1024)S(1)}, f32[1792,4]{0,1:T(4,128)S(1)}, f32[1792]{0:T(1024)S(1)}, f32[24]{0:T(128)S(1)}, f32[24]{0:T(128)S(1)}, /*index=5*/f32[24]{0:T(128)S(1)}, f32[1536]{0:T(1024)S(1)}) all-reduce(f32[768]{0:T(1024)S(1)} %get-tuple-element.104, ...), channel_id=1, replica_groups=mesh['fsdp'=2,'dp'=16] {'fsdp','dp'}, use_global_device_ids=true, to_apply=%region_58.59 | all-reduce | flops 11336 | bytes 90688 | tf_op jit(solution)/shard_map/psum | solution.py:194
  615.0 4.7 fusion.69
  619.7 7.0 fusion.144
  626.7 187.3 %all-reduce.39.cloned.1.call-done = (f32[768,3352]{0,1:T(8,128)}, f32[1536,768]{1,0:T(8,128)}) async-done(((f32[768,3352]{0,1:T(8,128)}, f32[1536,768]{1,0:T(8,128)}), (f32[768,3352]{0,1:T(8,128)}, f32[1536,768]{1,0:T(8,128)})) %all-reduce.39.cloned.1.call-update) | async-done | bytes 15015952 | tf_op jit(solution)/shard_map/psum | solution.py:194
  814.0 5.3 constant_dynamic-slice_fusion.2
  (550 shorter events, 210.2 us)
Async XLA Ops:
  7.2 9.8 %copy-start.141 = (bf16[384]{0:T(512)(128)(2,1)S(1)}, bf16[384]{0:T(512)(128)(2,1)}, u32[]{:S(2)}) copy-start(bf16[384]{0:T(512)(128)(2,1)} %param.14) | copy-start | bytes 2308
  7.2 13.1 %copy-start.138 = (bf16[768]{0:T(1024)(128)(2,1)S(1)}, bf16[768]{0:T(1024)(128)(2,1)}, u32[]{:S(2)}) copy-start(bf16[768]{0:T(1024)(128)(2,1)} %param.21) | copy-start | bytes 4612
  7.2 16.3 %copy-start.139 = (bf16[896]{0:T(1024)(128)(2,1)S(1)}, bf16[896]{0:T(1024)(128)(2,1)}, u32[]{:S(2)}) copy-start(bf16[896]{0:T(1024)(128)(2,1)} %param.17) | copy-start | bytes 5380
  7.3 20.3 %copy-start.21 = (bf16[1,1,1024,768]{3,2,1,0:T(8,128)(2,1)S(1)}, bf16[1,1,1024,768]{3,2,1,0:T(8,128)(2,1)}, u32[]{:S(2)}) copy-start(bf16[1,1,1024,768]{3,2,1,0:T(8,128)(2,1)} %param.12) | copy-start | bytes 4718596
  7.3 20.7 %copy-start.132 = (bf16[896,4]{0,1:T(4,128)(2,1)S(1)}, bf16[896,4]{0,1:T(4,128)(2,1)}, u32[]{:S(2)}) copy-start(bf16[896,4]{0,1:T(4,128)(2,1)} %param.16) | copy-start | bytes 21508
  7.3 72.3 %all-gather.6.cloned.1.call-start = ((), (), s32[]{:S(2)}) async-start(), calls=%async_computation | async-start | bytes 7723008 | tf_op jit(solution)/shard_map/all_gather | solution.py:127
  8.0 182.9 %all-gather.8.cloned.1.call-start = ((), (), s32[]{:S(2)}) async-start(), calls=%async_computation.1 | async-start | bytes 3538944 | tf_op jit(solution)/shard_map/all_gather | solution.py:134
  8.8 805.2 %all-reduce.39.cloned.1.call-start = ((), (), s32[]{:S(2)}) async-start(), calls=%async_computation.2 | async-start | bytes 30031872 | tf_op jit(solution)/shard_map/psum | solution.py:194
  16.5 76.5 %copy-start.134 = (f32[24]{0:T(128)}, f32[24]{0:T(128)S(1)}, u32[]{:S(2)}) copy-start(f32[24]{0:T(128)S(1)} %convert_element_type.73) | copy-start | bytes 292
  20.3 66.9 %copy-start.124 = (f32[768]{0:T(1024)}, f32[768]{0:T(1024)S(1)}, u32[]{:S(2)}) copy-start(f32[768]{0:T(1024)S(1)} %reshape.683) | copy-start | bytes 9220
  23.6 175.5 %copy-start.98 = (f32[1536]{0:T(1024)}, f32[1536]{0:T(1024)S(1)}, u32[]{:S(2)}) copy-start(f32[1536]{0:T(1024)S(1)} %reshape.684) | copy-start | bytes 18436
  27.9 59.4 %copy-start.96 = (f32[1024]{0:T(1024)}, f32[1024]{0:T(1024)S(1)}, u32[]{:S(2)}) copy-start(f32[1024]{0:T(1024)S(1)} %fusion.70) | copy-start | bytes 12292
  27.9 59.3 %copy-start.126 = (f32[1024]{0:T(1024)}, f32[1024]{0:T(1024)S(1)}, u32[]{:S(2)}) copy-start(f32[1024]{0:T(1024)S(1)} %fusion.305) | copy-start | bytes 12292
  31.7 76.5 %copy-start.85 = (f32[1792]{0:T(1024)}, f32[1792]{0:T(1024)S(1)}, u32[]{:S(2)}) copy-start(f32[1792]{0:T(1024)S(1)} %get-tuple-element.124) | copy-start | bytes 21508
  31.7 76.5 %copy-start.87 = (f32[1792]{0:T(1024)}, f32[1792]{0:T(1024)S(1)}, u32[]{:S(2)}) copy-start(f32[1792]{0:T(1024)S(1)} %get-tuple-element.125) | copy-start | bytes 21508
  31.8 76.5 %copy-start.89 = (f32[1792]{0:T(1024)}, f32[1792]{0:T(1024)S(1)}, u32[]{:S(2)}) copy-start(f32[1792]{0:T(1024)S(1)} %get-tuple-element.126) | copy-start | bytes 21508
  31.8 76.5 %copy-start.91 = (f32[1792]{0:T(1024)}, f32[1792]{0:T(1024)S(1)}, u32[]{:S(2)}) copy-start(f32[1792]{0:T(1024)S(1)} %get-tuple-element.127) | copy-start | bytes 21508
  93.0 15.2 %copy-start.33 = (f32[1024,24]{1,0:T(8,128)}, f32[1024,24]{1,0:T(8,128)S(1)}, u32[]{:S(2)}) copy-start(f32[1024,24]{1,0:T(8,128)S(1)} %copy.469) | copy-start | bytes 294916
  93.3 14.9 %copy-start.34 = (f32[1024,24]{1,0:T(8,128)}, f32[1024,24]{1,0:T(8,128)S(1)}, u32[]{:S(2)}) copy-start(f32[1024,24]{1,0:T(8,128)S(1)} %compare_select_fusion.2) | copy-start | bytes 294916
  97.6 10.6 %copy-start.50 = (f32[24,2,128]{0,2,1:T(8,128)}, f32[24,2,128]{0,2,1:T(8,128)S(1)}, u32[]{:S(2)}) copy-start(f32[24,2,128]{0,2,1:T(8,128)S(1)} %copy.313) | copy-start | bytes 73732
  99.8 8.4 %copy-start.51 = (f32[24,2,128]{0,2,1:T(8,128)}, f32[24,2,128]{0,2,1:T(8,128)S(1)}, u32[]{:S(2)}) copy-start(f32[24,2,128]{0,2,1:T(8,128)S(1)} %copy.322) | copy-start | bytes 73732
  108.2 17.0 %copy-start = (f32[1024,1792]{0,1:T(8,128)}, f32[1024,1792]{0,1:T(8,128)S(1)}, u32[]{:S(2)}) copy-start(f32[1024,1792]{0,1:T(8,128)S(1)} %slice.322) | copy-start | bytes 22020100
  117.7 7.6 copy-start.1
  125.2 8.7 %copy-start.133 = (f32[24]{0:T(128)S(1)}, f32[24]{0:T(128)}, u32[]{:S(2)}) copy-start(f32[24]{0:T(128)} %get-tuple-element.219) | copy-start | bytes 292
  127.4 34.9 %copy-start.6 = (f32[256,1536]{0,1:T(8,128)}, f32[256,1536]{0,1:T(8,128)S(1)}, u32[]{:S(2)}) copy-start(f32[256,1536]{0,1:T(8,128)S(1)} %get-tuple-element.170) | copy-start | bytes 4718596
  127.4 40.1 %copy-start.9 = (f32[256,1536]{0,1:T(8,128)}, f32[256,1536]{0,1:T(8,128)S(1)}, u32[]{:S(2)}) copy-start(f32[256,1536]{0,1:T(8,128)S(1)} %get-tuple-element.171) | copy-start | bytes 4718596
  136.0 13.6 %copy-start.144 = (f32[24]{0:T(128)S(1)}, f32[24]{0:T(128)}, u32[]{:S(2)}) copy-start(f32[24]{0:T(128)} %fusion.321) | copy-start | bytes 292
  162.3 15.9 %copy-start.25 = (f32[256,24,64]{0,2,1:T(8,128)}, f32[256,24,64]{0,2,1:T(8,128)S(1)}, u32[]{:S(2)}) copy-start(f32[256,24,64]{0,2,1:T(8,128)S(1)} %fusion.129) | copy-start | bytes 4718596
  167.5 10.7 %copy-start.27 = (f32[256,24,64]{0,2,1:T(8,128)}, f32[256,24,64]{0,2,1:T(8,128)S(1)}, u32[]{:S(2)}) copy-start(f32[256,24,64]{0,2,1:T(8,128)S(1)} %fusion.128) | copy-start | bytes 4718596
  178.2 8.1 copy-start.44
  190.9 8.2 copy-start.26
  190.9 8.2 copy-start.28
  190.9 8.2 copy-start.16
  190.9 8.2 copy-start.30
  190.9 8.2 copy-start.32
  190.9 8.2 copy-start.129
  214.2 9.4 %copy-start.37 = (f32[256,128]{0,1:T(8,128)S(1)}, f32[256,128]{0,1:T(8,128)}, u32[]{:S(2)}) copy-start(f32[256,128]{0,1:T(8,128)} %get-tuple-element.52) | copy-start | bytes 393220
  344.9 7.4 copy-start.8
  370.0 22.3 %copy-start.42 = (f32[256,128]{0,1:T(8,128)S(1)}, f32[256,128]{0,1:T(8,128)}, u32[]{:S(2)}) copy-start(f32[256,128]{0,1:T(8,128)} %get-tuple-element.76) | copy-start | bytes 393220
  370.0 22.3 %copy-start.61 = (f32[256,128]{0,1:T(8,128)S(1)}, f32[256,128]{0,1:T(8,128)}, u32[]{:S(2)}) copy-start(f32[256,128]{0,1:T(8,128)} %fusion.210) | copy-start | bytes 393220
  370.0 23.3 %copy-start.41 = (f32[256,128]{0,1:T(8,128)S(1)}, f32[256,128]{0,1:T(8,128)}, u32[]{:S(2)}) copy-start(f32[256,128]{0,1:T(8,128)} %get-tuple-element.74) | copy-start | bytes 393220
  370.0 24.3 %copy-start.38 = (f32[256,128]{0,1:T(8,128)S(1)}, f32[256,128]{0,1:T(8,128)}, u32[]{:S(2)}) copy-start(f32[256,128]{0,1:T(8,128)} %get-tuple-element.52) | copy-start | bytes 393220
  370.0 25.3 %copy-start.52 = (f32[256,128]{0,1:T(8,128)S(1)}, f32[256,128]{0,1:T(8,128)}, u32[]{:S(2)}) copy-start(f32[256,128]{0,1:T(8,128)} %get-tuple-element.51) | copy-start | bytes 393220
  370.0 25.3 %copy-start.60 = (f32[256,128]{0,1:T(8,128)S(1)}, f32[256,128]{0,1:T(8,128)}, u32[]{:S(2)}) copy-start(f32[256,128]{0,1:T(8,128)} %fusion.192) | copy-start | bytes 393220
  370.1 26.4 %copy-start.59 = (f32[24,2,128]{2,0,1:T(8,128)S(1)}, f32[24,2,128]{2,0,1:T(8,128)}, u32[]{:S(2)}) copy-start(f32[24,2,128]{2,0,1:T(8,128)} %reduce-window.94) | copy-start | bytes 73732
  370.1 26.3 %copy-start.84 = (f32[256,24]{0,1:T(8,128)S(1)}, f32[256,24]{0,1:T(8,128)}, u32[]{:S(2)}) copy-start(f32[256,24]{0,1:T(8,128)} %multiply_reduce_fusion.25) | copy-start | bytes 73732
  484.4 8.5 %copy-start.48 = (f32[256,24,64]{0,2,1:T(8,128)S(1)}, f32[256,24,64]{0,2,1:T(8,128)}, u32[]{:S(2)}) copy-start(f32[256,24,64]{0,2,1:T(8,128)} %get-tuple-element.215) | copy-start | bytes 4718596
  484.4 8.5 %copy-start.75 = (f32[256,256]{1,0:T(8,128)S(1)}, f32[256,256]{1,0:T(8,128)}, u32[]{:S(2)}) copy-start(f32[256,256]{1,0:T(8,128)} %fusion.337) | copy-start | bytes 786436
  484.4 8.5 %copy-start.80 = (f32[256,24]{0,1:T(8,128)S(1)}, f32[256,24]{0,1:T(8,128)}, u32[]{:S(2)}) copy-start(f32[256,24]{0,1:T(8,128)} %copy.370) | copy-start | bytes 73732
  484.4 8.5 %copy-start.95 = (pred[256,256]{1,0:T(8,128)(4,1)S(1)}, pred[256,256]{1,0:T(8,128)(4,1)}, u32[]{:S(2)}) copy-start(pred[256,256]{1,0:T(8,128)(4,1)} %iota_compare_fusion) | copy-start | bytes 196612
  484.4 8.5 %copy-start.101 = (f32[24,256]{1,0:T(8,128)S(1)}, f32[24,256]{1,0:T(8,128)}, u32[]{:S(2)}) copy-start(f32[24,256]{1,0:T(8,128)} %copy.347) | copy-start | bytes 73732
  484.4 8.5 %copy-start.107 = (f32[24,256]{1,0:T(8,128)S(1)}, f32[24,256]{1,0:T(8,128)}, u32[]{:S(2)}) copy-start(f32[24,256]{1,0:T(8,128)} %copy.346) | copy-start | bytes 73732
  484.4 8.5 %copy-start.153 = (f32[24]{0:T(128)S(1)}, f32[24]{0:T(128)}, u32[]{:S(2)}) copy-start(f32[24]{0:T(128)} %convert_element_type.75) | copy-start | bytes 292
  492.9 12.8 %slice-start.2 = ((s8[7340032]{0:T(1024)(128)(4,1)}), s8[4194304]{0:T(1024)(128)(4,1)S(1)}, s32[]{:S(2)}) async-start(s8[7340032]{0:T(1024)(128)(4,1)} %bitcast.539), calls=%async_computation.5 | async-start | bytes 8388608
  507.9 12.2 %copy-start.86 = (f32[1792]{0:T(1024)S(1)}, f32[1792]{0:T(1024)}, u32[]{:S(2)}) copy-start(f32[1792]{0:T(1024)} %copy-done.85) | copy-start | bytes 21508
  507.9 12.2 %copy-start.88 = (f32[1792]{0:T(1024)S(1)}, f32[1792]{0:T(1024)}, u32[]{:S(2)}) copy-start(f32[1792]{0:T(1024)} %copy-done.87) | copy-start | bytes 21508
  507.9 12.2 %copy-start.90 = (f32[1792]{0:T(1024)S(1)}, f32[1792]{0:T(1024)}, u32[]{:S(2)}) copy-start(f32[1792]{0:T(1024)} %copy-done.89) | copy-start | bytes 21508
  507.9 12.2 %copy-start.92 = (f32[1792]{0:T(1024)S(1)}, f32[1792]{0:T(1024)}, u32[]{:S(2)}) copy-start(f32[1792]{0:T(1024)} %copy-done.91) | copy-start | bytes 21508
  528.6 12.0 %copy-start.22 = (bf16[1,1,1024,768]{3,2,1,0:T(8,128)(2,1)S(1)}, bf16[1,1,1024,768]{3,2,1,0:T(8,128)(2,1)}, u32[]{:S(2)}) copy-start(bf16[1,1,1024,768]{3,2,1,0:T(8,128)(2,1)} %param.12) | copy-start | bytes 4718596
  528.6 12.0 %copy-start.125 = (f32[768]{0:T(1024)S(1)}, f32[768]{0:T(1024)}, u32[]{:S(2)}) copy-start(f32[768]{0:T(1024)} %copy-done.124) | copy-start | bytes 9220
  528.6 12.0 %copy-start.127 = (f32[1024]{0:T(1024)S(1)}, f32[1024]{0:T(1024)}, u32[]{:S(2)}) copy-start(f32[1024]{0:T(1024)} %copy-done.126) | copy-start | bytes 12292
  556.3 12.4 %copy-start.131 = (f32[1536]{0:T(1024)S(1)}, f32[1536]{0:T(1024)}, u32[]{:S(2)}) copy-start(f32[1536]{0:T(1024)} %get-tuple-element.84) | copy-start | bytes 18436
  556.3 58.7 %copy-start.97 = (f32[1024]{0:T(1024)S(1)}, f32[1024]{0:T(1024)}, u32[]{:S(2)}) copy-start(f32[1024]{0:T(1024)} %copy-done.96) | copy-start | bytes 12292
  556.3 58.7 %copy-start.45 = (bf16[1,1,1024,768]{3,2,1,0:T(8,128)(2,1)S(1)}, bf16[1,1,1024,768]{3,2,1,0:T(8,128)(2,1)}, u32[]{:S(2)}) copy-start(bf16[1,1,1024,768]{3,2,1,0:T(8,128)(2,1)} %param.23) | copy-start | bytes 4718596
  (97 other events, 503.3 us)
Sparse Core Ops, SparseCore 0:
  9.7 69.8 all-gather.5
  81.1 36.1 all-gather.7
  553.3 260.6 all-reduce.38
where the time goes:
time: 840 us; the launch traced here: 828 us
  waiting for transfers between devices  236 us (28%)
  matrix products  233 us (28%)
  other arithmetic  144 us (17%)
  local copies, waits for them, and re-layouts  135 us (16%)
  blocking collectives  60.2 us (7%)
  between operations  17.9 us (2%)
    psum x1, waiting for transfers between devices, shards(): lax.psum((d_gain, d_proj_weight, d_conv, d_shift, d_bias, d_rate, d_skip_...  187 us
    dot_general x12, matrix products, block_update(): jnp.einsum('hts,shp->thp', weights, value_block, precision=PRECISE)  87.6 us
    another operation x39, other arithmetic  63.8 us
    all_gather x1, waiting for transfers between devices, shards(): lax.all_gather(w_in, 'fsdp', axis=0, tiled=True)  47.8 us
    dot_general x15, matrix products, block_update(): jnp.einsum('hpn,tn->thp', state, c_block, precision=PRECISE)  43.3 us
    psum x1, blocking collectives, shards(): lax.psum((d_gain, d_proj_weight, d_conv, d_shift, d_bias, d_rate, d_skip_...  41.9 us
    another operation x50, local copies, waits for them, and re-layouts  40.3 us
    dot_general x9, matrix products, block_update(): jnp.einsum('shp,sn->hpn', scaled, b_block, precision=PRECISE)  27.9 us
  transfers between devices with their start and end apart: 3, of which 2 were waited for; matrix products, arithmetic and copies ran while one was open for 17% of the time, Pallas kernels for 0%

commit v1 on v0

v1 whole, which is shorter than its diff:
```python
import functools
import math

import jax
import jax.numpy as jnp
from jax import lax
from jax.experimental import pallas as pl
from jax.experimental.pallas import tpu as pltpu
from jax.sharding import PartitionSpec as P

EPSILON = 1e-05
LOG2E = math.log2(math.e)
SPAN = 256
STRETCH = 128
GROUP = 8
TILE = 256
LANES = 128
VMEM_LIMIT = 60 * 1024 * 1024

F32 = jnp.float32
BF16 = jnp.bfloat16


def mul_nn(a, b):
    return lax.dot_general(a, b, (((1,), (0,)), ((), ())), preferred_element_type=F32)


def mul_nt(a, b):
    return lax.dot_general(a, b, (((1,), (1,)), ((), ())), preferred_element_type=F32)


def mul_tn(a, b):
    return lax.dot_general(a, b, (((0,), (0,)), ((), ())), preferred_element_type=F32)


def triangle(size, keep):
    rows = lax.broadcasted_iota(jnp.int32, (size, size), 0)
    cols = lax.broadcasted_iota(jnp.int32, (size, size), 1)
    return keep(rows, cols)


def lane_sums(values, matrix):
    high = values.astype(BF16)
    rest = values - high.astype(F32)
    middle = rest.astype(BF16)
    low = (rest - middle.astype(F32)).astype(BF16)
    return mul_nn(high, matrix) + mul_nn(middle, matrix) + mul_nn(low, matrix)


def as_columns(rows):
    heads, span = rows.shape
    return jnp.concatenate([rows, jnp.zeros((LANES - heads, span), F32)], axis=0).T


def later(block, before, shift):
    lane = lax.broadcasted_iota(jnp.int32, (block.shape[0], LANES), 1)
    moved = pltpu.roll(block, shift, 1)
    first = jnp.where(lane < shift, pltpu.roll(before, shift, 1), moved[:, :LANES])
    if block.shape[1] == LANES:
        return first
    return jnp.concatenate([first, moved[:, LANES:]], axis=1)


def earlier(block, after, shift):
    span = block.shape[1]
    lane = lax.broadcasted_iota(jnp.int32, (block.shape[0], LANES), 1)
    moved = pltpu.roll(block, span - shift, 1)
    last = jnp.where(lane >= LANES - shift, pltpu.roll(after, LANES - shift, 1), moved[:, span - LANES :])
    if span == LANES:
        return last
    return jnp.concatenate([moved[:, : span - LANES], last], axis=1)


def fold(block):
    total = block[:, :LANES]
    for first in range(LANES, block.shape[1], LANES):
        total = total + block[:, first : first + LANES]
    return total


def softplus(v):
    return jnp.maximum(v, 0.0) + jnp.log1p(jnp.exp(-jnp.abs(v)))


def sigmoid(v):
    return 1.0 / (1.0 + jnp.exp(-v))


def decays(step, rate2):
    span = step.shape[1]
    upper = triangle(span, lambda r, c: r <= c).astype(BF16)
    cum = lane_sums(step * rate2, upper)
    total = cum[:, span - 1 : span]
    return cum, jnp.exp2(total - cum), jnp.exp2(cum), jnp.exp2(total)


def forward_body(
    sizes,
    skip_ref,
    alive_ref,
    tokens_ref,
    cotangent_ref,
    gain_ref,
    weight_ref,
    out_weight_ref,
    columns_ref,
    heads_ref,
    normed_ref,
    mixed_ref,
    active_ref,
    raw_ref,
    states_ref,
    low_mixed_ref,
    d_gate_ref,
    d_scan_ref,
    row_part_ref,
    skip_part_ref,
    gain_part_ref,
    state,
    tail,
    gate,
    scanned,
    carried,
    scaled,
    gated,
    d_normed,
    update,
    cum_s,
    step_s,
    factor_s,
    ec_s,
    total_s,
):
    inner, conv, heads, state_dim = sizes
    width = inner // heads
    span = tokens_ref.shape[0]
    stretch = min(STRETCH, span)

    @pl.when(pl.program_id(0) == 0)
    def _():
        state[...] = jnp.zeros_like(state)
        tail[...] = jnp.zeros_like(tail)
        gain_part_ref[...] = jnp.zeros_like(gain_part_ref)

    u = tokens_ref[...].astype(F32)
    normed = u * lax.rsqrt(jnp.mean(u * u, axis=1, keepdims=True) + EPSILON) * gain_ref[...]
    normed = normed.astype(BF16)
    normed_ref[...] = normed

    @pl.loop(0, inner // TILE)
    def _(i):
        rows = pl.ds(pl.multiple_of(i * TILE, TILE), TILE)
        gate[rows, :] = mul_nt(weight_ref[rows, :], normed)

    @pl.loop(0, conv // TILE)
    def _(i):
        rows = pl.ds(pl.multiple_of(i * TILE, TILE), TILE)
        block = mul_nt(weight_ref[pl.ds(pl.multiple_of(inner + i * TILE, TILE), TILE), :], normed)
        before = tail[rows, :]
        tail[rows, :] = block[:, span - LANES :]
        mixed_ref[rows, :] = block.astype(BF16)
        cols = columns_ref[rows, :]
        summed = cols[:, 4:5] + block * cols[:, 3:4]
        for shift in range(1, 4):
            summed = summed + later(block, before, shift) * cols[:, 3 - shift : 4 - shift]
        active_ref[rows, :] = (summed * sigmoid(summed)).astype(BF16)

    raw = mul_nt(weight_ref[inner + conv : inner + conv + 32, :], normed)[:heads] + heads_ref[:, 0:1]
    raw_ref[...] = raw
    step_all = softplus(raw)
    rate2 = -jnp.exp(heads_ref[:, 1:2]) * LOG2E
    causal = triangle(stretch, lambda r, c: r <= c)
    for part in range(span // stretch):
        lanes = slice(part * stretch, (part + 1) * stretch)
        step = step_all[:, lanes]
        cum, factor, ec, total = decays(step, rate2)
        cum_s[...] = cum
        step_s[...] = step
        factor_s[...] = factor * step
        ec_s[...] = ec
        total_s[...] = jnp.broadcast_to(total, (heads, LANES))
        b_in = active_ref[inner : inner + state_dim, lanes]
        c_in = active_ref[inner + state_dim : inner + 2 * state_dim, lanes]
        scores = jnp.where(causal, mul_tn(b_in, c_in), 0.0)
        low_state = state[...].astype(BF16)
        states_ref[part] = low_state
        carried[...] = mul_nn(low_state, c_in)

        @pl.loop(0, heads // GROUP)
        def _(group):
            eight = pl.ds(pl.multiple_of(group * GROUP, GROUP), GROUP)
            cum_g, step_g, factor_g, ec_g = cum_s[eight, :], step_s[eight, :], factor_s[eight, :], ec_s[eight, :]
            cum_c = as_columns(cum_g)
            for j in range(GROUP):
                rows = pl.ds(pl.multiple_of((group * GROUP + j) * width, width), width)
                row = slice(j, j + 1)
                values = active_ref[rows, lanes].astype(F32)
                stepped = (values * step_g[row]).astype(BF16)
                decay = jnp.exp2(jnp.minimum(cum_g[row] - cum_c[:, row], 0.0))
                weights = (scores * decay).astype(BF16)
                scanned[rows, lanes] = mul_nn(stepped, weights) + ec_g[row] * carried[rows, :]
                scaled[rows, :] = (values * factor_g[row]).astype(BF16)

        update[...] = mul_nt(scaled[...], b_in)

        @pl.loop(0, heads // GROUP)
        def _(group):
            eight = pl.ds(pl.multiple_of(group * GROUP, GROUP), GROUP)
            total_g = total_s[eight, :]
            for j in range(GROUP):
                rows = pl.ds(pl.multiple_of((group * GROUP + j) * width, width), width)
                state[rows, :] = total_g[j : j + 1] * state[rows, :] + update[rows, :]

    def gated_head(h, squares):
        rows = pl.ds(pl.multiple_of(h * width, width), width)
        z = gate[rows, :]
        y = scanned[rows, :] + skip_ref[h] * active_ref[rows, :].astype(F32)
        v = y * (z * sigmoid(z))
        gated[rows, :] = v
        return squares + (v * v).reshape(width // 8, 8, span).sum(axis=0)

    squares = lax.fori_loop(0, heads, gated_head, jnp.zeros((8, span), F32))
    scale = lax.rsqrt(jnp.sum(squares, axis=0, keepdims=True) / inner + EPSILON)
    incoming = (cotangent_ref[...].astype(F32) * alive_ref[0]).astype(BF16)

    def norm_tile(i, dots):
        rows = pl.ds(pl.multiple_of(i * TILE, TILE), TILE)
        gain = columns_ref[rows, 5:6]
        unit = gated[rows, :] * scale
        low_mixed_ref[rows, :] = (unit * gain).astype(BF16)
        d_mixed = mul_nt(out_weight_ref[rows, :], incoming)
        gain_part_ref[rows, :] += fold(d_mixed * unit)
        d_unit = d_mixed * gain
        d_normed[rows, :] = d_unit
        return dots + (d_unit * unit).reshape(TILE // 8, 8, span).sum(axis=0)

    dots = lax.fori_loop(0, inner // TILE, norm_tile, jnp.zeros((8, span), F32))
    mean_dot = jnp.sum(dots, axis=0, keepdims=True) / inner

    @pl.loop(0, heads // GROUP)
    def _(group):
        eight = pl.ds(pl.multiple_of(group * GROUP, GROUP), GROUP)
        row_parts, skip_parts = [], []
        for j in range(GROUP):
            h = group * GROUP + j
            rows = pl.ds(pl.multiple_of(h * width, width), width)
            z = gate[rows, :]
            sig = sigmoid(z)
            values = active_ref[rows, :].astype(F32)
            pure = scanned[rows, :]
            y = pure + skip_ref[h] * values
            d_gated = scale * (d_normed[rows, :] - gated[rows, :] * (scale * mean_dot))
            d_scan = (d_gated * (z * sig)).astype(BF16)
            d_scan_ref[rows, :] = d_scan
            d_gate_ref[rows, :] = (d_gated * y * (sig * (1.0 + z * (1.0 - sig)))).astype(BF16)
            d_scan = d_scan.astype(F32)
            row_parts.append(jnp.sum(d_scan * pure, axis=0, keepdims=True))
            skip_parts.append(jnp.sum(d_scan * values, axis=0, keepdims=True))
        row_part_ref[eight, :] = jnp.concatenate(row_parts, axis=0)
        skip_part_ref[eight, :] = jnp.concatenate(skip_parts, axis=0)


def backward_body(
    sizes,
    skip_ref,
    active_ref,
    mixed_ref,
    before_ref,
    d_scan_ref,
    raw_ref,
    row_part_ref,
    states_ref,
    columns_ref,
    heads_ref,
    d_rest_ref,
    d_raw_ref,
    rate_part_ref,
    conv_part_ref,
    d_state,
    carry,
    d_active,
    sums,
    from_state,
    scaled,
    d_scaled,
    d_scores,
    state_dots,
    cum_s,
    step_s,
    factor_s,
    ec_s,
    total_s,
    pair_s,
    direct_s,
    ending_s,
):
    inner, conv, heads, state_dim = sizes
    width = inner // heads
    span = active_ref.shape[1]
    stretch = min(STRETCH, span)
    first_block = pl.program_id(0) == pl.num_programs(0) - 1

    @pl.when(pl.program_id(0) == 0)
    def _():
        d_state[...] = jnp.zeros_like(d_state)
        carry[...] = jnp.zeros_like(carry)
        sums[...] = jnp.zeros_like(sums)

    raw = raw_ref[...]
    step_all = softplus(raw)
    slope = sigmoid(raw)
    rate = -jnp.exp(heads_ref[:, 1:2])
    rate2 = rate * LOG2E
    causal = triangle(stretch, lambda r, c: r <= c)
    ending = triangle(stretch, lambda r, c: r >= c).astype(BF16)
    before_it = triangle(stretch, lambda r, c: r < c).astype(BF16)
    for part in reversed(range(span // stretch)):
        lanes = slice(part * stretch, (part + 1) * stretch)
        step = step_all[:, lanes]
        cum, factor, ec, total = decays(step, rate2)
        cum_s[...] = cum
        step_s[...] = step
        factor_s[...] = factor
        ec_s[...] = ec
        total_s[...] = jnp.broadcast_to(total, (heads, LANES))
        b_in = active_ref[inner : inner + state_dim, lanes]
        c_in = active_ref[inner + state_dim : inner + 2 * state_dim, lanes]
        scores = jnp.where(causal, mul_tn(b_in, c_in), 0.0)
        low_d_state = d_state[...].astype(BF16)
        from_state[...] = mul_nn(low_d_state, b_in)
        d_scores[...] = jnp.zeros_like(d_scores)

        @pl.loop(0, heads // GROUP)
        def _(group):
            eight = pl.ds(pl.multiple_of(group * GROUP, GROUP), GROUP)
            cum_g, step_g, factor_g, ec_g = cum_s[eight, :], step_s[eight, :], factor_s[eight, :], ec_s[eight, :]
            cum_c = as_columns(cum_g)
            pairs, directs, endings, dots = [], [], [], []
            d_scores_g = d_scores[...]
            for j in range(GROUP):
                h = group * GROUP + j
                rows = pl.ds(pl.multiple_of(h * width, width), width)
                row = slice(j, j + 1)
                values = active_ref[rows, lanes].astype(F32)
                stepped = (values * step_g[row]).astype(BF16)
                low_d = d_scan_ref[rows, lanes]
                d_scan = low_d.astype(F32)
                decay = jnp.exp2(jnp.minimum(cum_g[row] - cum_c[:, row], 0.0))
                weights = (scores * decay).astype(BF16)
                inside = mul_nt(low_d, weights)
                d_scores_g = d_scores_g + mul_tn(stepped, low_d) * decay
                across = from_state[rows, :] * factor_g[row]
                both = inside + across
                d_active[rows, lanes] = step_g[row] * both + skip_ref[h] * d_scan
                pairs.append(jnp.sum(stepped.astype(F32) * inside, axis=0, keepdims=True))
                directs.append(jnp.sum(values * both, axis=0, keepdims=True))
                endings.append(jnp.sum(values * across, axis=0, keepdims=True))
                scaled[rows, :] = (values * (step_g[row] * factor_g[row])).astype(BF16)
                d_scaled[rows, :] = (d_scan * ec_g[row]).astype(BF16)
                dots.append(jnp.sum(d_state[rows, :] * states_ref[part, rows, :].astype(F32), axis=0, keepdims=True))
            d_scores[...] = d_scores_g
            pair_s[eight, :] = jnp.concatenate(pairs, axis=0)
            direct_s[eight, :] = jnp.concatenate(directs, axis=0)
            ending_s[eight, :] = jnp.concatenate(endings, axis=0)
            state_dots[eight, :] = jnp.concatenate(dots, axis=0)

        low_d_scores = jnp.where(causal, d_scores[...], 0.0).astype(BF16)
        low_state = states_ref[part]
        d_active[inner : inner + state_dim, lanes] = mul_tn(low_d_state, scaled[...]) + mul_nt(c_in, low_d_scores)
        d_active[inner + state_dim : inner + 2 * state_dim, lanes] = mul_tn(low_state, d_scaled[...]) + mul_nn(
            b_in, low_d_scores
        )
        from_state[...] = mul_nt(d_scaled[...], c_in)

        @pl.loop(0, heads // GROUP)
        def _(group):
            eight = pl.ds(pl.multiple_of(group * GROUP, GROUP), GROUP)
            total_g = total_s[eight, :]
            for j in range(GROUP):
                rows = pl.ds(pl.multiple_of((group * GROUP + j) * width, width), width)
                d_state[rows, :] = total_g[j : j + 1] * d_state[rows, :] + from_state[rows, :]

        d_log = (
            lane_sums(row_part_ref[:, lanes] - pair_s[...], ending)
            + lane_sums(step * ending_s[...], before_it)
            + total * jnp.sum(state_dots[...], axis=1, keepdims=True)
        )
        rate_part_ref[:, lanes] = d_log * step * rate
        d_raw_ref[:, lanes] = (direct_s[...] + d_log * rate) * slope[:, lanes]

    @pl.loop(0, conv // TILE)
    def _(i):
        rows = pl.ds(pl.multiple_of(i * TILE, TILE), TILE)
        block = mixed_ref[rows, :].astype(F32)
        before = jnp.where(first_block, 0.0, before_ref[rows, :].astype(F32))
        cols = columns_ref[rows, :]
        moved = [block] + [later(block, before, shift) for shift in range(1, 4)]
        summed = cols[:, 4:5] + block * cols[:, 3:4]
        for shift in range(1, 4):
            summed = summed + moved[shift] * cols[:, 3 - shift : 4 - shift]
        sig = sigmoid(summed)
        d_summed = d_active[rows, :] * (sig * (1.0 + summed * (1.0 - sig)))
        after = carry[rows, :]
        carry[rows, :] = d_summed[:, :LANES]
        d_block = d_summed * cols[:, 3:4]
        for shift in range(1, 4):
            d_block = d_block + earlier(d_summed, after, shift) * cols[:, 3 - shift : 4 - shift]
        d_rest_ref[rows, :] = d_block.astype(BF16)
        for shift in range(4):
            sums[3 - shift, rows, :] += fold(d_summed * moved[shift])
        sums[4, rows, :] += fold(d_summed)

    @pl.when(first_block)
    def _():
        @pl.loop(0, conv // TILE)
        def _(i):
            rows = pl.ds(pl.multiple_of(i * TILE, TILE), TILE)
            lane = lax.broadcasted_iota(jnp.int32, (TILE, LANES), 1)
            result = jnp.zeros((TILE, LANES), F32)
            for k in range(5):
                result = jnp.where(lane == k, jnp.sum(sums[k, rows, :], axis=1, keepdims=True), result)
            conv_part_ref[rows, :] = result


def whole(shape):
    return pl.BlockSpec(shape, lambda c: (0,) * len(shape), pipeline_mode=pl.Buffered(1))


def forward(sizes, skip, alive, tokens, cotangent, gain, weight, out_weight, columns, heads_in):
    inner, conv, heads, state_dim = sizes
    length, model = tokens.shape
    span = min(SPAN, length)
    stretch = min(STRETCH, span)
    parts = span // stretch
    smem = pl.BlockSpec(memory_space=pltpu.SMEM)
    along = lambda rows: pl.BlockSpec((rows, span), lambda c: (0, c))
    down = pl.BlockSpec((span, model), lambda c: (c, 0))
    shape = jax.ShapeDtypeStruct
    return pl.pallas_call(
        functools.partial(forward_body, sizes),
        grid=(length // span,),
        in_specs=[
            smem,
            smem,
            down,
            down,
            whole(gain.shape),
            whole(weight.shape),
            whole(out_weight.shape),
            whole(columns.shape),
            whole(heads_in.shape),
        ],
        out_specs=[
            down,
            along(conv),
            along(conv),
            along(heads),
            pl.BlockSpec((parts, inner, state_dim), lambda c: (c, 0, 0)),
            along(inner),
            along(inner),
            along(inner),
            along(heads),
            along(heads),
            pl.BlockSpec((inner, LANES), lambda c: (0, 0)),
        ],
        out_shape=[
            shape((length, model), BF16),
            shape((conv, length), BF16),
            shape((conv, length), BF16),
            shape((heads, length), F32),
            shape((length // stretch, inner, state_dim), BF16),
            shape((inner, length), BF16),
            shape((inner, length), BF16),
            shape((inner, length), BF16),
            shape((heads, length), F32),
            shape((heads, length), F32),
            shape((inner, LANES), F32),
        ],
        scratch_shapes=[
            pltpu.VMEM((inner, state_dim), F32),
            pltpu.VMEM((conv, LANES), F32),
            pltpu.VMEM((inner, span), F32),
            pltpu.VMEM((inner, span), F32),
            pltpu.VMEM((inner, stretch), F32),
            pltpu.VMEM((inner, stretch), BF16),
            pltpu.VMEM((inner, span), F32),
            pltpu.VMEM((inner, span), F32),
            pltpu.VMEM((inner, state_dim), F32),
            pltpu.VMEM((heads, stretch), F32),
            pltpu.VMEM((heads, stretch), F32),
            pltpu.VMEM((heads, stretch), F32),
            pltpu.VMEM((heads, stretch), F32),
            pltpu.VMEM((heads, LANES), F32),
        ],
        compiler_params=pltpu.CompilerParams(
            dimension_semantics=("arbitrary",), vmem_limit_bytes=VMEM_LIMIT
        ),
        name="block_forward",
    )(skip, alive, tokens, cotangent, gain, weight, out_weight, columns, heads_in)


def backward(sizes, skip, active, mixed, d_scan, raw, row_part, states, columns, heads_in):
    inner, conv, heads, state_dim = sizes
    length = active.shape[1]
    span = min(SPAN, length)
    stretch = min(STRETCH, span)
    parts = span // stretch
    blocks = length // span
    per = span // LANES
    smem = pl.BlockSpec(memory_space=pltpu.SMEM)
    along = lambda rows: pl.BlockSpec((rows, span), lambda c: (0, blocks - 1 - c))
    shape = jax.ShapeDtypeStruct
    return pl.pallas_call(
        functools.partial(backward_body, sizes),
        grid=(blocks,),
        in_specs=[
            smem,
            along(conv),
            along(conv),
            pl.BlockSpec((conv, LANES), lambda c: (0, jnp.maximum((blocks - 1 - c) * per - 1, 0))),
            along(inner),
            along(heads),
            along(heads),
            pl.BlockSpec((parts, inner, state_dim), lambda c: (blocks - 1 - c, 0, 0)),
            whole(columns.shape),
            whole(heads_in.shape),
        ],
        out_specs=[
            along(conv),
            along(heads),
            along(heads),
            pl.BlockSpec((conv, LANES), lambda c: (0, 0)),
        ],
        out_shape=[
            shape((conv, length), BF16),
            shape((heads, length), F32),
            shape((heads, length), F32),
            shape((conv, LANES), F32),
        ],
        scratch_shapes=[
            pltpu.VMEM((inner, state_dim), F32),
            pltpu.VMEM((conv, LANES), F32),
            pltpu.VMEM((conv, span), F32),
            pltpu.VMEM((5, conv, LANES), F32),
            pltpu.VMEM((inner, stretch), F32),
            pltpu.VMEM((inner, stretch), BF16),
            pltpu.VMEM((inner, stretch), BF16),
            pltpu.VMEM((stretch, stretch), F32),
            pltpu.VMEM((heads, state_dim), F32),
            pltpu.VMEM((heads, stretch), F32),
            pltpu.VMEM((heads, stretch), F32),
            pltpu.VMEM((heads, stretch), F32),
            pltpu.VMEM((heads, stretch), F32),
            pltpu.VMEM((heads, LANES), F32),
            pltpu.VMEM((heads, stretch), F32),
            pltpu.VMEM((heads, stretch), F32),
            pltpu.VMEM((heads, stretch), F32),
        ],
        compiler_params=pltpu.CompilerParams(
            dimension_semantics=("arbitrary",), vmem_limit_bytes=VMEM_LIMIT
        ),
        name="block_backward",
    )(skip, active, mixed, mixed, d_scan, raw, row_part, states, columns, heads_in)


def powers_of_two(size):
    bits, bit = [], 1
    while bit < size:
        bits.append(bit)
        bit *= 2
    return bits if bit == size else None


def swap(block, axis, bit):
    pairs = [(k, k ^ bit) for k in range(lax.axis_size(axis))]
    return lax.ppermute(block, axis, pairs)


def halves(block, side):
    rows = block.shape[0] // 2
    keep = lax.dynamic_slice_in_dim(block, side * rows, rows, 0)
    give = lax.dynamic_slice_in_dim(block, (1 - side) * rows, rows, 0)
    return keep, give


def halve(block, axis, bit):
    side = (lax.axis_index(axis) // bit) % 2
    keep, give = halves(block, side)
    return (keep.astype(F32) + swap(give, axis, bit).astype(F32)).astype(block.dtype)


def double(block, axis, bit):
    side = (lax.axis_index(axis) // bit) % 2
    other = swap(block, axis, bit)
    return jnp.where(
        side == 0, jnp.concatenate([block, other], axis=0), jnp.concatenate([other, block], axis=0)
    )


def summed_share(parts):
    groups = parts.shape[0]
    owner_bits, copy_bits = powers_of_two(lax.axis_size("fsdp")), powers_of_two(lax.axis_size("dp"))
    if owner_bits is None or copy_bits is None or parts.shape[1] % (8 * lax.axis_size("dp")):
        total = lax.psum(parts, ("fsdp", "dp"))
        return lax.dynamic_index_in_dim(total, lax.axis_index("fsdp"), 0, False).astype(F32)
    rows, columns = parts.shape[1:]
    block = parts.transpose(1, 0, 2)
    for bit in copy_bits[:1]:
        block = halve(block, "dp", bit)
    block = block.transpose(1, 0, 2)
    for bit in reversed(owner_bits):
        block = halve(block, "fsdp", bit)
    block = block[0]
    for bit in copy_bits[1:]:
        block = halve(block, "dp", bit)
    for bit in reversed(copy_bits):
        block = double(block, "dp", bit)
    return block.astype(F32)


def gathered_rows(block):
    groups, copies = lax.axis_size("fsdp"), lax.axis_size("dp")
    rows = block.shape[0]
    if groups != 2 or copies % 2 or rows % 32:
        return lax.all_gather(block, "fsdp")
    core = lax.axis_index("dp") % 2
    keep, _ = halves(block, core)
    direct = swap(keep, "fsdp", 1)
    relayed = swap(direct, "dp", 1)
    other = jnp.where(
        core == 0, jnp.concatenate([direct, relayed], axis=0), jnp.concatenate([relayed, direct], axis=0)
    )
    mine = lax.axis_index("fsdp")
    return jnp.where(mine == 0, jnp.stack([block, other]), jnp.stack([other, block]))


def shards(
    tokens,
    live,
    norm_gain,
    w_in,
    conv_weight,
    conv_bias,
    dt_bias,
    a_log,
    d_skip,
    inner_gain,
    w_out,
    cotangent,
):
    groups = lax.axis_size("fsdp")
    conv_each, inner_each, model_each, heads_each = (
        conv_weight.shape[0],
        inner_gain.shape[0],
        norm_gain.shape[0],
        dt_bias.shape[0],
    )
    conv, inner, heads = conv_each * groups, inner_each * groups, heads_each * groups
    model = tokens.shape[-1]
    proj = w_in.shape[1]
    sizes = (inner, conv, heads, (conv - inner) // 2)
    rows_padded = -(-proj // 32) * 32

    small_each = jnp.concatenate([norm_gain, dt_bias, a_log, d_skip])
    line = max(conv_each, inner_each, small_each.shape[0])
    fit = lambda v: jnp.pad(v, (0, line - v.shape[0]))[None]
    packed = jnp.concatenate(
        [jnp.pad(conv_weight.T, ((0, 0), (0, line - conv_each))), fit(conv_bias), fit(inner_gain), fit(small_each)],
        axis=0,
    )
    small = lax.all_gather(packed, "fsdp").astype(F32)
    taps = conv_weight.shape[1]
    lined = lambda k, first, each: small[:, k, first : first + each].reshape(1, groups * each)
    gain = lined(taps + 2, 0, model_each)
    first = model_each
    step_bias, log_rate, skip = [lined(taps + 2, first + k * heads_each, heads_each)[0] for k in range(3)]
    columns = jnp.concatenate(
        [lined(k, 0, conv_each) for k in range(taps + 1)]
        + [jnp.pad(lined(taps + 1, 0, inner_each), ((0, 0), (0, conv - inner))), jnp.zeros((2, conv), F32)],
        axis=0,
    ).T
    heads_in = jnp.stack([step_bias, log_rate], axis=1)

    weight = gathered_rows(jnp.pad(w_in.T, ((0, rows_padded - proj), (0, 0))))
    weight = weight.transpose(1, 0, 2).reshape(rows_padded, model)
    out_weight = gathered_rows(w_out).reshape(inner, model)

    alive = live.astype(F32).reshape(1)
    low_tokens, low_cotangent = tokens[0, 0], cotangent[0, 0]
    (
        normed,
        mixed,
        active,
        raw,
        states,
        low_mixed,
        d_gate,
        d_scan,
        row_part,
        skip_part,
        gain_part,
    ) = forward(sizes, skip, alive, low_tokens, low_cotangent, gain, weight, out_weight, columns, heads_in)
    u = low_tokens.astype(F32)
    incoming = low_cotangent.astype(F32) * alive[0]
    low_incoming = incoming.astype(BF16)

    def owned(left):
        product = mul_nn(left, normed).astype(BF16)
        return product.reshape(left.shape[0], groups, model_each).transpose(1, 0, 2)

    out_parts = mul_nn(low_mixed, low_incoming).astype(BF16).reshape(groups, inner_each, model)
    g_out = summed_share(out_parts)
    g_gate = summed_share(owned(d_gate))

    d_rest, d_raw, rate_part, conv_part = backward(
        sizes, skip, active, mixed, d_scan, raw, row_part, states, columns, heads_in
    )
    spare = -(-(proj - inner) // (16 * lax.axis_size("dp"))) * 16 * lax.axis_size("dp") - conv - heads
    d_rest = jnp.concatenate([d_rest, d_raw.astype(BF16), jnp.zeros((spare, d_raw.shape[1]), BF16)], axis=0)
    g_rest = summed_share(owned(d_rest))[: proj - inner]

    block_out = (alive[0] * (u + mul_tn(low_mixed, out_weight))).astype(BF16)
    d_normed = mul_tn(d_gate, weight[:inner]) + mul_tn(d_rest[: proj - inner], weight[inner:proj])
    scale = lax.rsqrt(jnp.mean(u * u, axis=1, keepdims=True) + EPSILON)
    unit = u * scale
    d_unit = d_normed * gain
    input_grad = incoming + scale * (d_unit - unit * jnp.mean(d_unit * unit, axis=1, keepdims=True))

    small_grads = (
        jnp.sum(d_normed * unit, axis=0),
        conv_part[:, :taps],
        conv_part[:, taps],
        jnp.sum(d_raw, axis=1),
        jnp.sum(rate_part, axis=1),
        jnp.sum(skip_part, axis=1),
        jnp.sum(gain_part, axis=1),
    )
    totals = lax.psum(small_grads, ("fsdp", "dp"))
    owner = lax.axis_index("fsdp")
    g_gain, g_conv, g_shift, g_bias, g_rate, g_skip, g_inner = [
        lax.dynamic_slice_in_dim(total, owner * (total.shape[0] // groups), total.shape[0] // groups, 0)
        for total in totals
    ]
    g_proj = jnp.concatenate([g_gate, g_rest], axis=0).T
    return (
        block_out.reshape(tokens.shape),
        input_grad.reshape(cotangent.shape),
        g_gain,
        g_proj,
        g_conv,
        g_shift,
        g_bias,
        g_rate,
        g_skip,
        g_inner,
        g_out,
    )


def solution(mesh):
    by_device = P("fsdp", "dp", None, None)
    lines, tables = P("fsdp"), P("fsdp", None)
    return jax.shard_map(
        shards,
        mesh=mesh,
        in_specs=(
            by_device,
            P("fsdp", "dp"),
            lines,
            tables,
            tables,
            lines,
            lines,
            lines,
            lines,
            lines,
            tables,
            by_device,
        ),
        out_specs=(by_device, by_device, lines, tables, tables, lines, lines, lines, lines, lines, tables),
        check_vma=False,
    )
```

time: 840 us -> 438 us (0.52)
  matrix products: 233 us -> 34.5 us
  waiting for transfers between devices: 236 us -> 60.3 us
  Pallas kernels: 0 us -> 132 us
  other arithmetic: 144 us -> 30.9 us
  local copies, waits for them, and re-layouts: 135 us -> 47.5 us
  starting transfers between devices: 0.11 us -> 36.8 us
  blocking collectives: 60.2 us -> 89.3 us
  between operations: 17.9 us -> 2.47 us
    dot_general x58 -> x6, matrix products: 233 us -> 34.5 us  [the longest x3 17.4 us: mul_nn(): lax.dot_general(a, b, (((1,), (0,)), ((), ())), preferred_element_type=F32)]
    psum x1 -> x0, waiting for transfers between devices: 187 us -> none  [shards(): lax.psum((d_gain, d_proj_weight, d_conv, d_shift, d_bias, d_rate, d_skip_...]
    pallas_call x0 -> x2, Pallas kernels: none -> 132 us  [the longest x1 75.3 us: forward(): pl.pallas_call(functools.partial(forward_body, sizes), grid=(length // sp...]
    another operation x39 -> x1, other arithmetic: 63.8 us -> 0.01 us  [shards(): heads_in = jnp.stack([step_bias, log_rate], axis=1)]
    ppermute x0 -> x31, waiting for transfers between devices: none -> 60.3 us  [swap(): return lax.ppermute(block, axis, pairs)]
    all_gather x2 -> x0, waiting for transfers between devices: 47.8 us -> none  [the longest x1 47.8 us: shards(): lax.all_gather(w_in, 'fsdp', axis=0, tiled=True)]
    another operation x50 -> x5, local copies, waits for them, and re-layouts: 40.3 us -> 3.12 us  [the longest x1 1.69 us: gathered_rows(): jnp.stack([block, other])]
    ppermute x0 -> x31, starting transfers between devices: none -> 36.8 us  [swap(): return lax.ppermute(block, axis, pairs)]
  transfers between devices with their start and end apart: 3 -> 31, of which waited for: 2 -> 10; matrix products, arithmetic and copies ran while one was open for 17% -> 14% of each run, Pallas kernels for 0% -> 0%
where the time goes in v1:
time: 438 us; the launch traced here: 434 us
  Pallas kernels  132 us (30%)
  blocking collectives  89.3 us (20%)
  waiting for transfers between devices  60.3 us (14%)
  local copies, waits for them, and re-layouts  47.5 us (11%)
  starting transfers between devices  36.8 us (8%)
  matrix products  34.5 us (8%)
  other arithmetic  30.9 us (7%)
    pallas_call x1, Pallas kernels, forward(): pl.pallas_call(functools.partial(forward_body, sizes), grid=(length // sp...  75.3 us
    ppermute x31, waiting for transfers between devices, swap(): return lax.ppermute(block, axis, pairs)  60.3 us
    pallas_call x1, Pallas kernels, backward(): pl.pallas_call(functools.partial(backward_body, sizes), grid=(blocks,), i...  56.8 us
    psum x1, blocking collectives, shards(): totals = lax.psum(small_grads, ('fsdp', 'dp'))  50.2 us
    all_gather x1, blocking collectives, shards(): small = lax.all_gather(packed, 'fsdp').astype(F32)  39.1 us
    ppermute x31, starting transfers between devices, swap(): return lax.ppermute(block, axis, pairs)  36.8 us
    dot_general x3, matrix products, mul_nn(): lax.dot_general(a, b, (((1,), (0,)), ((), ())), preferred_element_type=F32)  17.4 us
    dot_general x3, matrix products, mul_tn(): lax.dot_general(a, b, (((0,), (0,)), ((), ())), preferred_element_type=F32)  17.1 us
  transfers between devices with their start and end apart: 31, of which 10 were waited for; matrix products, arithmetic and copies ran while one was open for 14% of the time, Pallas kernels for 0%

profile of v1, /device:TPU:1, one launch (start us, length us, event | category | flops | bytes accessed | tf_op | source)
XLA Modules:
  0.0 433.8 jit_solution(8571354316813137957)
XLA Ops:
  0.7 3.3 copy.46
  4.0 1.7 pad_dynamic-slice_fusion
  5.7 2.5 copy.47
  8.2 2.0 collective-permute-start
  10.3 1.9 constant_dynamic-slice_fusion.11
  12.4 39.1 %all-gather.1 = bf16[2,7,896]{2,1,0:T(8,128)(2,1)S(1)} all-gather(bf16[1,7,896]{2,1,0:T(8,128)(2,1)S(1)} %maximum_bitcast_fusion), channel_id=2, replica_groups=mesh['fsdp'=2,'dp'=16] {'fsdp'}, dimensions={0}, use_global_device_ids=true | all-gather | bytes 37632 | tf_op jit(solution)/shard_map/all_gather | solution.py:671
  51.5 1.8 fusion.23
  53.3 1.3 collective-permute-start.1
  57.1 0.7 copy.52.heads_ref
  57.9 1.3 copy.51
  59.3 1.7 pad_bitcast_fusion
  61.0 1.7 maximum_select_fusion.3
  62.7 1.8 maximum_select_fusion.2
  64.4 3.0 copy.48
  67.5 2.5 copy.49
  70.0 5.1 %maximum_select_fusion.1 = bf16[1,3360,384]{1,2,0:T(8,128)(2,1)S(1)} fusion(bf16[1,1680,384]{1,2,0:T(8,128)(2,1)} %bitcast.107, bf16[1,1680,384]{1,2,0:T(8,128)(2,1)} %bitcast.106, pred[]{:T(512)S(6)} %eq.57), kind=kLoop, calls=%fused_computation.32 | loop fusion | flops 11612160 | bytes 5160961 | tf_op jit(solution)/shard_map/jit(_where)/select_n | solution.py:630
  75.1 1.1 fusion.59
  76.2 4.0 maximum_select_fusion
  80.3 8.0 %copy.59.weight_ref = bf16[3360,768]{1,0:T(8,128)(2,1)} copy(bf16[3360,768]{0,1:T(8,128)(2,1)} %bitcast.97) | data formatting | bytes 10321920 | tf_op jit(solution)/shard_map/reshape | solution.py:685
  88.2 75.3 %block_forward.1 = (bf16[1024,768]{1,0:T(8,128)(2,1)}, bf16[1792,1024]{1,0:T(8,128)(2,1)}, bf16[1792,1024]{1,0:T(8,128)(2,1)}, f32[24,1024]{1,0:T(8,128)}, bf16[...) custom-call(f32[24]{0:T(128)} %squeeze_reshape_squeeze.3.skip_ref, ...), custom_call_target="tpu_custom_call" | custom-call | tf_op jit(solution)/shard_map/block_forward/pallas_call | solution.py:439
  163.6 56.8 %block_backward.1 = (bf16[1792,1024]{1,0:T(8,128)(2,1)}, f32[24,1024]{1,0:T(8,128)}, f32[24,1024]{1,0:T(8,128)}, f32[1792,128]{1,0:T(8,128)}) custom-call(f32[24]{0:T(128)} %squeeze_reshape_squeeze.3.skip_ref, bf16[1792,1024]{1,0:T(8,128)(2,1)} %get-tuple-element.28.active_ref, bf16[1792,1024]{1,0:T(8,128)(2,1)} %get-tuple-element.29.mixed_ref.before_ref, ...), custom_call_target="tpu_custom_call" | custom-call | tf_op jit(solution)/shard_map/block_backward/pallas_call | solution.py:513
  220.3 1.1 fusion.48
  221.5 5.1 %convolution_convert_fusion.1 = bf16[1536,768]{0,1:T(8,128)(2,1)S(1)} fusion(bf16[1536,1024]{1,0:T(8,128)(2,1)} %get-tuple-element.27, bf16[1024,768]{1,0:T(8,128)(2,1)S(1)} %copy-done.24), kind=kOutput, calls=%fused_computation.18 | convolution fusion | flops 2417098752 | bytes 7077888 | tf_op jit(solution)/shard_map/dot_general | solution.py:25
  226.6 5.3 %fusion.8 = f32[1024,768]{1,0:T(8,128)} fusion(bf16[1816,768]{0,1:T(8,128)(2,1)S(1)} %bitcast.99, bf16[24,1024]{1,0:T(8,128)(2,1)S(1)} %get-tuple-element.91, bf16[1792,1024]{1,0:T(8,128)(2,1)S(1)} %copy-done.22), kind=kOutput, calls=%fused_computation.13 | convolution fusion | flops 2863759360 | bytes 9654272 | tf_op jit(solution)/shard_map/dot_general | solution.py:33
  231.9 5.8 %fusion.12 = bf16[2048,768]{0,1:T(8,128)(2,1)} fusion(bf16[1024,768]{1,0:T(8,128)(2,1)S(1)} %copy-done.24, bf16[24,1024]{1,0:T(8,128)(2,1)S(1)} %get-tuple-element.91, bf16[1792,1024]{1,0:T(8,128)(2,1)S(1)} %copy-done.22, bf16[2048]{0:T(1024)(128)(2,1)S(1)} %pad.56.clone), kind=kOutput, calls=%fused_computation.19 | convolution fusion | flops 3235381248 | bytes 8441856 | tf_op jit(solution)/shard_map/dot_general | solution.py:25
  237.6 1.2 constant_dynamic-slice_fusion.10
  238.8 1.6 copy.61
  241.0 6.5 %convolution_convert_fusion = bf16[1536,768]{1,0:T(8,128)(2,1)} fusion(bf16[1536,1024]{1,0:T(8,128)(2,1)} %get-tuple-element.26, f32[]{:T(128)} %bitcast, bf16[1,1,1024,768]{3,2,1,0:T(8,128)(2,1)} %param.23), kind=kOutput, calls=%fused_computation.17 | convolution fusion | flops 2419458048 | bytes 7077892 | tf_op jit(solution)/shard_map/dot_general | solution.py:25
  247.5 5.2 %fusion.20 = (f32[768]{0:T(1024)S(1)}, f32[1024]{0:T(1024)S(1)}, f32[1024,768]{1,0:T(8,128)}) fusion(f32[1024]{0:T(1024)S(1)} %add_rsqrt_fusion, bf16[1,1,1024,768]{3,2,1,0:T(8,128)(2,1)S(1)} %copy-done.2, f32[768]{0:T(1024)S(1)} %mul.149, f32[1024,768]{1,0:T(8,128)S(1)} %copy-done.25, bf16[1536,1024]{1,0:T(8,128)(2,1)S(1)} %copy-done.23, ...), kind=kOutput, calls=%fused_computation.25 | convolution fusion | flops 2422208768 | bytes 13383680 | tf_op jit(solution)/shard_map/dot_general | solution.py:33
  252.8 1.5 constant_dynamic-slice_fusion.6
  254.8 1.6 copy.62
  256.4 2.4 copy.60
  259.4 50.2 %all-reduce.4 = (f32[768]{0:T(1024)S(1)}, f32[1792,4]{1,0:T(8,128)S(1)}, f32[1792]{0:T(1024)S(1)}, f32[24]{0:T(128)S(1)}, f32[24]{0:T(128)S(1)}, /*index=5*/f32[24]{0:T(128)S(1)}, f32[1536]{0:T(1024)S(1)}) all-reduce(f32[768]{0:T(1024)S(1)} %get-tuple-element.74, ...), channel_id=1, replica_groups=mesh['fsdp'=2,'dp'=16] {'fsdp','dp'}, use_global_device_ids=true, to_apply=%region_3.4 | all-reduce | flops 11336 | bytes 90688 | tf_op jit(solution)/shard_map/psum | solution.py:738
  312.1 0.8 copy.58
  312.8 2.5 dynamic-slice_bitcast_fusion
  315.3 2.4 collective-permute-start.22
  317.7 2.8 copy.63
  321.9 6.6 %fusion.30 = bf16[1,1,1024,768]{3,2,1,0:T(8,128)(2,1)} fusion(bf16[1536,1024]{1,0:T(8,128)(2,1)} %get-tuple-element.26, bf16[1536,768]{1,0:T(8,128)(2,1)} %bitcast.102, f32[]{:T(128)} %bitcast, bf16[1,1,1024,768]{3,2,1,0:T(8,128)(2,1)S(1)} %copy-done.3), kind=kOutput, calls=%fused_computation.44 | convolution fusion | flops 2419064832 | bytes 8650756 | tf_op jit(solution)/shard_map/dot_general | solution.py:33
  328.5 1.7 add_convert_fusion.1
  330.7 1.7 fusion.25
  332.5 1.1 collective-permute-start.23
  334.6 10.3 %collective-permute-done.5 = bf16[1,768,384]{2,1,0:T(8,128)(2,1)S(1)} collective-permute-done((bf16[1,768,384]{2,1,0:T(8,128)(2,1)S(1)}, bf16[1,768,384]{2,1,0:T(8,128)(2,1)S(1)}, u32[]{:S(2)}, u32[]{:S(2)}) %collective-permute-start.5) | collective-permute-done | bytes 589856 | tf_op jit(solution)/shard_map/ppermute | solution.py:576
  345.4 12.1 %collective-permute-done.23 = bf16[1,384,768]{2,1,0:T(8,128)(2,1)S(1)} collective-permute-done((bf16[1,384,768]{2,1,0:T(8,128)(2,1)S(1)}, bf16[1,384,768]{2,1,0:T(8,128)(2,1)S(1)}, u32[]{:S(2)}, u32[]{:S(2)}) %collective-permute-start.23) | collective-permute-done | bytes 589856 | tf_op jit(solution)/shard_map/ppermute | solution.py:576
  358.1 1.1 collective-permute-start.7
  359.3 4.7 %collective-permute-done.24 = bf16[192,768]{1,0:T(8,128)(2,1)S(1)} collective-permute-done((bf16[192,768]{1,0:T(8,128)(2,1)S(1)}, bf16[192,768]{1,0:T(8,128)(2,1)S(1)}, u32[]{:S(2)}, u32[]{:S(2)}) %collective-permute-start.24) | collective-permute-done | bytes 294944 | tf_op jit(solution)/shard_map/ppermute | solution.py:576
  364.1 0.8 collective-permute-start.25
  365.0 1.1 collective-permute-start.8
  366.1 8.2 %collective-permute-done.14 = bf16[1,1024,384]{2,1,0:T(8,128)(2,1)S(1)} collective-permute-done((bf16[1,1024,384]{2,1,0:T(8,128)(2,1)S(1)}, bf16[1,1024,384]{2,1,0:T(8,128)(2,1)S(1)}, u32[]{:S(2)}, u32[]{:S(2)}) %collective-permute-start.14) | collective-permute-done | bytes 786464 | tf_op jit(solution)/shard_map/ppermute | solution.py:576
  375.0 1.9 collective-permute-start.26
  377.5 6.4 %collective-permute-done.15 = bf16[512,384]{1,0:T(8,128)(2,1)S(1)} collective-permute-done((bf16[512,384]{1,0:T(8,128)(2,1)S(1)}, bf16[512,384]{1,0:T(8,128)(2,1)S(1)}, u32[]{:S(2)}, u32[]{:S(2)}) %collective-permute-start.15) | collective-permute-done | bytes 393248 | tf_op jit(solution)/shard_map/ppermute | solution.py:576
  384.1 0.8 collective-permute-start.16
  384.9 1.2 collective-permute-start.27
  386.1 3.8 collective-permute-done.16
  390.8 4.9 %collective-permute-done.17 = bf16[128,384]{1,0:T(8,128)(2,1)S(1)} collective-permute-done((bf16[128,384]{1,0:T(8,128)(2,1)S(1)}, bf16[128,384]{1,0:T(8,128)(2,1)S(1)}, u32[]{:S(2)}, u32[]{:S(2)}) %collective-permute-start.17) | collective-permute-done | bytes 98336 | tf_op jit(solution)/shard_map/ppermute | solution.py:576
  395.8 1.7 collective-permute-start.28
  397.5 3.4 collective-permute-done.18
  401.6 0.9 collective-permute-done.28
  402.8 5.5 %collective-permute-done.19 = bf16[256,384]{1,0:T(8,128)(2,1)S(1)} collective-permute-done((bf16[256,384]{1,0:T(8,128)(2,1)S(1)}, bf16[256,384]{1,0:T(8,128)(2,1)S(1)}, u32[]{:S(2)}, u32[]{:S(2)}) %collective-permute-start.19) | collective-permute-done | bytes 196640 | tf_op jit(solution)/shard_map/ppermute | solution.py:576
  408.8 7.4 %collective-permute-start.12 = (bf16[768,384]{1,0:T(8,128)(2,1)S(1)}, bf16[768,384]{1,0:T(8,128)(2,1)S(1)}, u32[]{:S(2)}, u32[]{:S(2)}) collective-permute-start(bf16[768,384]{1,0:T(8,128)(2,1)S(1)} %maximum_select_fusion.7), channel_id=1, source_target_pairs={{0,1},{1,0},{2,3},{3,2},{4,5},{5,4},{6,7},{7,6},{8,9},{9,8},{10,11... | collective-permute-start | bytes 1769480 | tf_op jit(solution)/shard_map/ppermute | solution.py:576
  416.4 5.0 %collective-permute-start.30 = (bf16[384,768]{1,0:T(8,128)(2,1)S(1)}, bf16[384,768]{1,0:T(8,128)(2,1)S(1)}, u32[]{:S(2)}, u32[]{:S(2)}) collective-permute-start(bf16[384,768]{1,0:T(8,128)(2,1)S(1)} %maximum_select_fusion.8), channel_id=1, source_target_pairs={{0,1},{1,0},{2,3},{3,2},{4,5},{5,4},{6,7},{7,6},{8,9},{9,8},{10,11... | collective-permute-start | bytes 1769480 | tf_op jit(solution)/shard_map/ppermute | solution.py:576
  421.7 4.0 collective-permute-start.21
  425.8 2.7 fusion.19
  428.4 1.7 fusion.32
  430.9 2.7 convert_bitcast_fusion
  (165 shorter events, 15.4 us)
Async XLA Ops:
  5.7 6.5 %copy-start.18 = (bf16[384]{0:T(512)(128)(2,1)S(1)}, bf16[384]{0:T(512)(128)(2,1)}, u32[]{:S(2)}) copy-start(bf16[384]{0:T(512)(128)(2,1)} %param.14) | copy-start | bytes 2308
  5.7 6.6 %copy-start.19 = (bf16[12]{0:T(256)(128)(2,1)S(1)}, bf16[12]{0:T(256)(128)(2,1)}, u32[]{:S(2)}) copy-start(bf16[12]{0:T(256)(128)(2,1)} %param.20) | copy-start | bytes 76
  5.7 6.6 %copy-start.20 = (bf16[12]{0:T(256)(128)(2,1)S(1)}, bf16[12]{0:T(256)(128)(2,1)}, u32[]{:S(2)}) copy-start(bf16[12]{0:T(256)(128)(2,1)} %param.19) | copy-start | bytes 76
  5.7 6.6 %copy-start.21 = (bf16[12]{0:T(256)(128)(2,1)S(1)}, bf16[12]{0:T(256)(128)(2,1)}, u32[]{:S(2)}) copy-start(bf16[12]{0:T(256)(128)(2,1)} %param.18) | copy-start | bytes 76
  5.7 6.7 %copy-start.16 = (bf16[768]{0:T(1024)(128)(2,1)S(1)}, bf16[768]{0:T(1024)(128)(2,1)}, u32[]{:S(2)}) copy-start(bf16[768]{0:T(1024)(128)(2,1)} %param.21) | copy-start | bytes 4612
  5.7 6.7 %copy-start.17 = (bf16[896]{0:T(1024)(128)(2,1)S(1)}, bf16[896]{0:T(1024)(128)(2,1)}, u32[]{:S(2)}) copy-start(bf16[896]{0:T(1024)(128)(2,1)} %param.17) | copy-start | bytes 5380
  5.7 6.7 %copy-start.15 = (bf16[896,4]{0,1:T(4,128)(2,1)S(1)}, bf16[896,4]{0,1:T(4,128)(2,1)}, u32[]{:S(2)}) copy-start(bf16[896,4]{0,1:T(4,128)(2,1)} %param.16) | copy-start | bytes 21508
  8.2 45.1 %collective-permute-start = (bf16[1680,384]{1,0:T(8,128)(2,1)}, bf16[1680,384]{1,0:T(8,128)(2,1)}, u32[]{:S(2)}, u32[]{:S(2)}) collective-permute-start(bf16[1680,384]{1,0:T(8,128)(2,1)} %copy.47), channel_id=1, source_target_pairs={{0,16},{16,0},{1,17},{17,1},{2,18},{18,2},{3,19},{19,3},{4,20},{20... | collective-permute-start | bytes 3870728 | tf_op jit(solution)/shard_map/ppermute | solution.py:576
  12.2 44.8 %collective-permute-start.2 = (bf16[384,768]{1,0:T(8,128)(2,1)}, bf16[384,768]{1,0:T(8,128)(2,1)S(1)}, u32[]{:S(2)}, u32[]{:S(2)}) collective-permute-start(bf16[384,768]{1,0:T(8,128)(2,1)} %constant_dynamic-slice_fusion.11), channel_id=1, source_target_pairs={{0,16},{16,0},{1,17},{17,1},{2,18},{18,2},{3,19},{19,3},{4,20},{20... | collective-permute-start | bytes 1769480 | tf_op jit(solution)/shard_map/ppermute | solution.py:576
  53.3 14.1 %collective-permute-start.1 = (bf16[1680,384]{1,0:T(8,128)(2,1)}, bf16[1680,384]{1,0:T(8,128)(2,1)}, u32[]{:S(2)}, u32[]{:S(2)}) collective-permute-start(bf16[1680,384]{1,0:T(8,128)(2,1)} %collective-permute-done), channel_id=1, source_target_pairs={{0,1},{1,0},{2,3},{3,2},{4,5},{5,4},{6,7},{7,6},{8,9},{9,8},{10,11... | collective-permute-start | bytes 3870728 | tf_op jit(solution)/shard_map/ppermute | solution.py:576
  57.0 4.0 collective-permute-start.3
  61.0 1.7 copy-start.10
  70.0 5.1 %copy-start = (bf16[1,3360,384]{1,2,0:T(8,128)(2,1)S(1)}, bf16[1,3360,384]{1,2,0:T(8,128)(2,1)}, u32[]{:S(2)}) copy-start(bf16[1,3360,384]{1,2,0:T(8,128)(2,1)} %pad_bitcast_fusion) | copy-start | bytes 7741444
  76.2 4.1 copy-start.1
  163.5 57.9 %copy-start.24 = (bf16[1024,768]{1,0:T(8,128)(2,1)S(1)}, bf16[1024,768]{1,0:T(8,128)(2,1)}, u32[]{:S(2)}) copy-start(bf16[1024,768]{1,0:T(8,128)(2,1)} %get-tuple-element.36) | copy-start | bytes 4718596
  221.4 5.2 %slice-start.1 = ((bf16[3360,2,384]{0,2,1:T(8,128)(2,1)}), bf16[1816,2,384]{0,2,1:T(8,128)(2,1)S(1)}, s32[]{:S(2)}) async-start(bf16[3360,2,384]{0,2,1:T(8,128)(2,1)} %copy-done.1), calls=%async_computation.1 | async-start | bytes 5898240 | tf_op jit(solution)/shard_map/slice | solution.py:723
  221.4 5.2 %copy-start.22 = (bf16[1792,1024]{1,0:T(8,128)(2,1)S(1)}, bf16[1792,1024]{1,0:T(8,128)(2,1)}, u32[]{:S(2)}) copy-start(bf16[1792,1024]{1,0:T(8,128)(2,1)} %get-tuple-element.34) | copy-start | bytes 11010052
  240.4 88.1 %collective-permute-start.4 = (bf16[768,2,384]{2,0,1:T(8,128)(2,1)}, bf16[768,2,384]{2,0,1:T(8,128)(2,1)}, u32[]{:S(2)}, u32[]{:S(2)}) collective-permute-start(bf16[768,2,384]{2,0,1:T(8,128)(2,1)} %copy.61), channel_id=1, source_target_pairs={{0,1},{1,0},{2,3},{3,2},{4,5},{5,4},{6,7},{7,6},{8,9},{9,8},{10,11... | collective-permute-start | bytes 3538952 | tf_op jit(solution)/shard_map/ppermute | solution.py:576
  240.9 6.5 %slice-start = ((bf16[3360,2,384]{0,2,1:T(8,128)(2,1)}), bf16[1536,2,384]{0,2,1:T(8,128)(2,1)S(1)}, s32[]{:S(2)}) async-start(bf16[3360,2,384]{0,2,1:T(8,128)(2,1)} %copy-done.1), calls=%async_computation | async-start | bytes 4718592 | tf_op jit(solution)/shard_map/slice | solution.py:723
  240.9 6.6 %copy-start.2 = (bf16[1,1,1024,768]{3,2,1,0:T(8,128)(2,1)S(1)}, bf16[1,1,1024,768]{3,2,1,0:T(8,128)(2,1)}, u32[]{:S(2)}) copy-start(bf16[1,1,1024,768]{3,2,1,0:T(8,128)(2,1)} %param.12) | copy-start | bytes 4718596
  240.9 6.6 %copy-start.23 = (bf16[1536,1024]{1,0:T(8,128)(2,1)S(1)}, bf16[1536,1024]{1,0:T(8,128)(2,1)}, u32[]{:S(2)}) copy-start(bf16[1536,1024]{1,0:T(8,128)(2,1)} %get-tuple-element.27) | copy-start | bytes 9437188
  241.0 6.6 %copy-start.25 = (f32[1024,768]{1,0:T(8,128)S(1)}, f32[1024,768]{1,0:T(8,128)}, u32[]{:S(2)}) copy-start(f32[1024,768]{1,0:T(8,128)} %fusion.8) | copy-start | bytes 9437188
  247.5 5.2 %copy-start.9 = (bf16[2048,768]{0,1:T(8,128)(2,1)S(1)}, bf16[2048,768]{0,1:T(8,128)(2,1)}, u32[]{:S(2)}) copy-start(bf16[2048,768]{0,1:T(8,128)(2,1)} %fusion.12) | copy-start | bytes 9437188
  252.8 1.5 copy-start.14
  252.8 1.6 copy-start.13
  252.8 1.7 copy-start.12
  254.8 4.0 copy-start.7
  312.8 9.1 %copy-start.3 = (bf16[1,1,1024,768]{3,2,1,0:T(8,128)(2,1)S(1)}, bf16[1,1,1024,768]{3,2,1,0:T(8,128)(2,1)}, u32[]{:S(2)}) copy-start(bf16[1,1,1024,768]{3,2,1,0:T(8,128)(2,1)} %param.12) | copy-start | bytes 4718596
  315.3 15.4 %collective-permute-start.22 = (bf16[384,2,768]{2,0,1:T(8,128)(2,1)}, bf16[384,2,768]{2,0,1:T(8,128)(2,1)}, u32[]{:S(2)}, u32[]{:S(2)}) collective-permute-start(bf16[384,2,768]{2,0,1:T(8,128)(2,1)} %dynamic-slice_bitcast_fusion), channel_id=1, source_target_pairs={{0,1},{1,0},{2,3},{3,2},{4,5},{5,4},{6,7},{7,6},{8,9},{9,8},{10,11... | collective-permute-start | bytes 3538952 | tf_op jit(solution)/shard_map/ppermute | solution.py:576
  320.5 13.1 %collective-permute-start.13 = (bf16[1024,2,384]{2,0,1:T(8,128)(2,1)}, bf16[1024,2,384]{2,0,1:T(8,128)(2,1)S(1)}, u32[]{:S(2)}, u32[]{:S(2)}) collective-permute-start(bf16[1024,2,384]{2,0,1:T(8,128)(2,1)} %copy.63), channel_id=1, source_target_pairs={{0,1},{1,0},{2,3},{3,2},{4,5},{5,4},{6,7},{7,6},{8,9},{9,8},{10,11... | collective-permute-start | bytes 4718600 | tf_op jit(solution)/shard_map/ppermute | solution.py:576
  321.9 6.6 %copy-start.6 = (bf16[768,2,384]{2,0,1:T(8,128)(2,1)S(1)}, bf16[768,2,384]{2,0,1:T(8,128)(2,1)}, u32[]{:S(2)}) copy-start(bf16[768,2,384]{2,0,1:T(8,128)(2,1)} %copy.60) | copy-start | bytes 3538948
  328.5 2.2 copy-start.11
  330.4 3.3 copy-start.4
  330.4 14.5 %collective-permute-start.5 = (bf16[1,768,384]{2,1,0:T(8,128)(2,1)S(1)}, bf16[1,768,384]{2,1,0:T(8,128)(2,1)S(1)}, u32[]{:S(2)}, u32[]{:S(2)}) collective-permute-start(bf16[1,768,384]{2,1,0:T(8,128)(2,1)S(1)} %dynamic-slice_bitcast_fusion.3), channel_id=1, source_target_pairs={{0,16},{16,0},{1,17},{17,1},{2,18},{18,2},{3,19},{19,3},{4,20},{20... | collective-permute-start | bytes 1769480 | tf_op jit(solution)/shard_map/ppermute | solution.py:576
  332.5 25.0 %collective-permute-start.23 = (bf16[1,384,768]{2,1,0:T(8,128)(2,1)S(1)}, bf16[1,384,768]{2,1,0:T(8,128)(2,1)S(1)}, u32[]{:S(2)}, u32[]{:S(2)}) collective-permute-start(bf16[1,384,768]{2,1,0:T(8,128)(2,1)S(1)} %dynamic-slice_bitcast_fusion.2), channel_id=1, source_target_pairs={{0,16},{16,0},{1,17},{17,1},{2,18},{18,2},{3,19},{19,3},{4,20},{20... | collective-permute-start | bytes 1769480 | tf_op jit(solution)/shard_map/ppermute | solution.py:576
  334.1 40.2 %collective-permute-start.14 = (bf16[1,1024,384]{2,1,0:T(8,128)(2,1)S(1)}, bf16[1,1024,384]{2,1,0:T(8,128)(2,1)S(1)}, u32[]{:S(2)}, u32[]{:S(2)}) collective-permute-start(bf16[1,1024,384]{2,1,0:T(8,128)(2,1)S(1)} %dynamic-slice_bitcast_fusion.1), channel_id=1, source_target_pairs={{0,16},{16,0},{1,17},{17,1},{2,18},{18,2},{3,19},{19,3},{4,20},{20... | collective-permute-start | bytes 2359304 | tf_op jit(solution)/shard_map/ppermute | solution.py:576
  345.0 13.0 %collective-permute-start.6 = (bf16[384,384]{1,0:T(8,128)(2,1)S(1)}, bf16[384,384]{1,0:T(8,128)(2,1)S(1)}, u32[]{:S(2)}, u32[]{:S(2)}) collective-permute-start(bf16[384,384]{1,0:T(8,128)(2,1)S(1)} %dynamic-slice_bitcast_fusion.6), channel_id=1, source_target_pairs={{0,2},{1,3},{2,0},{3,1},{4,6},{5,7},{6,4},{7,5},{8,10},{9,11},{10,... | collective-permute-start | bytes 884744 | tf_op jit(solution)/shard_map/ppermute | solution.py:576
  357.7 6.3 %collective-permute-start.24 = (bf16[192,768]{1,0:T(8,128)(2,1)S(1)}, bf16[192,768]{1,0:T(8,128)(2,1)S(1)}, u32[]{:S(2)}, u32[]{:S(2)}) collective-permute-start(bf16[192,768]{1,0:T(8,128)(2,1)S(1)} %dynamic-slice_bitcast_fusion.5), channel_id=1, source_target_pairs={{0,2},{1,3},{2,0},{3,1},{4,6},{5,7},{6,4},{7,5},{8,10},{9,11},{10,... | collective-permute-start | bytes 884744 | tf_op jit(solution)/shard_map/ppermute | solution.py:576
  358.1 6.8 %collective-permute-start.7 = (bf16[192,384]{1,0:T(8,128)(2,1)S(1)}, bf16[192,384]{1,0:T(8,128)(2,1)S(1)}, u32[]{:S(2)}, u32[]{:S(2)}) collective-permute-start(bf16[192,384]{1,0:T(8,128)(2,1)S(1)} %constant_dynamic-slice_fusion.8), channel_id=1, source_target_pairs={{0,4},{1,5},{2,6},{3,7},{4,0},{5,1},{6,2},{7,3},{8,12},{9,13},{10,... | collective-permute-start | bytes 442376 | tf_op jit(solution)/shard_map/ppermute | solution.py:576
  364.1 10.9 %collective-permute-start.25 = (bf16[96,768]{1,0:T(8,128)(2,1)S(1)}, bf16[96,768]{1,0:T(8,128)(2,1)S(1)}, u32[]{:S(2)}, u32[]{:S(2)}) collective-permute-start(bf16[96,768]{1,0:T(8,128)(2,1)S(1)} %constant_dynamic-slice_fusion.1), channel_id=1, source_target_pairs={{0,4},{1,5},{2,6},{3,7},{4,0},{5,1},{6,2},{7,3},{8,12},{9,13},{10,... | collective-permute-start | bytes 442376 | tf_op jit(solution)/shard_map/ppermute | solution.py:576
  365.0 11.9 %collective-permute-start.8 = (bf16[96,384]{1,0:T(8,128)(2,1)S(1)}, bf16[96,384]{1,0:T(8,128)(2,1)S(1)}, u32[]{:S(2)}, u32[]{:S(2)}) collective-permute-start(bf16[96,384]{1,0:T(8,128)(2,1)S(1)} %constant_dynamic-slice_fusion.7), channel_id=1, source_target_pairs={{0,8},{1,9},{2,10},{3,11},{4,12},{5,13},{6,14},{7,15},{8,0},{9,1},... | collective-permute-start | bytes 221192 | tf_op jit(solution)/shard_map/ppermute | solution.py:576
  374.6 9.3 %collective-permute-start.15 = (bf16[512,384]{1,0:T(8,128)(2,1)S(1)}, bf16[512,384]{1,0:T(8,128)(2,1)S(1)}, u32[]{:S(2)}, u32[]{:S(2)}) collective-permute-start(bf16[512,384]{1,0:T(8,128)(2,1)S(1)} %dynamic-slice_bitcast_fusion.4), channel_id=1, source_target_pairs={{0,2},{1,3},{2,0},{3,1},{4,6},{5,7},{6,4},{7,5},{8,10},{9,11},{10,... | collective-permute-start | bytes 1179656 | tf_op jit(solution)/shard_map/ppermute | solution.py:576
  375.0 9.9 %collective-permute-start.26 = (bf16[48,768]{1,0:T(8,128)(2,1)S(1)}, bf16[48,768]{1,0:T(8,128)(2,1)S(1)}, u32[]{:S(2)}, u32[]{:S(2)}) collective-permute-start(bf16[48,768]{1,0:T(8,128)(2,1)S(1)} %constant_dynamic-slice_fusion), channel_id=1, source_target_pairs={{0,8},{1,9},{2,10},{3,11},{4,12},{5,13},{6,14},{7,15},{8,0},{9,1},... | collective-permute-start | bytes 221192 | tf_op jit(solution)/shard_map/ppermute | solution.py:576
  376.9 13.4 %collective-permute-start.9 = (bf16[96,384]{1,0:T(8,128)(2,1)S(1)}, bf16[96,384]{1,0:T(8,128)(2,1)S(1)}, u32[]{:S(2)}, u32[]{:S(2)}) collective-permute-start(bf16[96,384]{1,0:T(8,128)(2,1)S(1)} %add_convert_fusion.7), channel_id=1, source_target_pairs={{0,8},{1,9},{2,10},{3,11},{4,12},{5,13},{6,14},{7,15},{8,0},{9,1},... | collective-permute-start | bytes 221192 | tf_op jit(solution)/shard_map/ppermute | solution.py:576
  384.1 5.8 %collective-permute-start.16 = (bf16[256,384]{1,0:T(8,128)(2,1)S(1)}, bf16[256,384]{1,0:T(8,128)(2,1)S(1)}, u32[]{:S(2)}, u32[]{:S(2)}) collective-permute-start(bf16[256,384]{1,0:T(8,128)(2,1)S(1)} %constant_dynamic-slice_fusion.4), channel_id=1, source_target_pairs={{0,4},{1,5},{2,6},{3,7},{4,0},{5,1},{6,2},{7,3},{8,12},{9,13},{10,... | collective-permute-start | bytes 589832 | tf_op jit(solution)/shard_map/ppermute | solution.py:576
  384.9 10.8 %collective-permute-start.27 = (bf16[48,768]{1,0:T(8,128)(2,1)S(1)}, bf16[48,768]{1,0:T(8,128)(2,1)S(1)}, u32[]{:S(2)}, u32[]{:S(2)}) collective-permute-start(bf16[48,768]{1,0:T(8,128)(2,1)S(1)} %add_convert_fusion.6), channel_id=1, source_target_pairs={{0,8},{1,9},{2,10},{3,11},{4,12},{5,13},{6,14},{7,15},{8,0},{9,1},... | collective-permute-start | bytes 221192 | tf_op jit(solution)/shard_map/ppermute | solution.py:576
  390.0 5.7 %collective-permute-start.17 = (bf16[128,384]{1,0:T(8,128)(2,1)S(1)}, bf16[128,384]{1,0:T(8,128)(2,1)S(1)}, u32[]{:S(2)}, u32[]{:S(2)}) collective-permute-start(bf16[128,384]{1,0:T(8,128)(2,1)S(1)} %constant_dynamic-slice_fusion.3), channel_id=1, source_target_pairs={{0,8},{1,9},{2,10},{3,11},{4,12},{5,13},{6,14},{7,15},{8,0},{9,1},... | collective-permute-start | bytes 294920 | tf_op jit(solution)/shard_map/ppermute | solution.py:576
  390.3 10.7 %collective-permute-start.10 = (bf16[192,384]{1,0:T(8,128)(2,1)S(1)}, bf16[192,384]{1,0:T(8,128)(2,1)S(1)}, u32[]{:S(2)}, u32[]{:S(2)}) collective-permute-start(bf16[192,384]{1,0:T(8,128)(2,1)S(1)} %maximum_select_fusion.13), channel_id=1, source_target_pairs={{0,4},{1,5},{2,6},{3,7},{4,0},{5,1},{6,2},{7,3},{8,12},{9,13},{10,... | collective-permute-start | bytes 442376 | tf_op jit(solution)/shard_map/ppermute | solution.py:576
  395.7 5.2 %collective-permute-start.18 = (bf16[128,384]{1,0:T(8,128)(2,1)S(1)}, bf16[128,384]{1,0:T(8,128)(2,1)S(1)}, u32[]{:S(2)}, u32[]{:S(2)}) collective-permute-start(bf16[128,384]{1,0:T(8,128)(2,1)S(1)} %add_convert_fusion.5), channel_id=1, source_target_pairs={{0,8},{1,9},{2,10},{3,11},{4,12},{5,13},{6,14},{7,15},{8,0},{9,1},... | collective-permute-start | bytes 294920 | tf_op jit(solution)/shard_map/ppermute | solution.py:576
  395.8 6.7 %collective-permute-start.28 = (bf16[96,768]{1,0:T(8,128)(2,1)S(1)}, bf16[96,768]{1,0:T(8,128)(2,1)S(1)}, u32[]{:S(2)}, u32[]{:S(2)}) collective-permute-start(bf16[96,768]{1,0:T(8,128)(2,1)S(1)} %maximum_select_fusion.14), channel_id=1, source_target_pairs={{0,4},{1,5},{2,6},{3,7},{4,0},{5,1},{6,2},{7,3},{8,12},{9,13},{10,... | collective-permute-start | bytes 442376 | tf_op jit(solution)/shard_map/ppermute | solution.py:576
  400.9 7.4 %collective-permute-start.19 = (bf16[256,384]{1,0:T(8,128)(2,1)S(1)}, bf16[256,384]{1,0:T(8,128)(2,1)S(1)}, u32[]{:S(2)}, u32[]{:S(2)}) collective-permute-start(bf16[256,384]{1,0:T(8,128)(2,1)S(1)} %maximum_select_fusion.12), channel_id=1, source_target_pairs={{0,4},{1,5},{2,6},{3,7},{4,0},{5,1},{6,2},{7,3},{8,12},{9,13},{10,... | collective-permute-start | bytes 589832 | tf_op jit(solution)/shard_map/ppermute | solution.py:576
  401.1 7.4 %collective-permute-start.11 = (bf16[384,384]{1,0:T(8,128)(2,1)S(1)}, bf16[384,384]{1,0:T(8,128)(2,1)S(1)}, u32[]{:S(2)}, u32[]{:S(2)}) collective-permute-start(bf16[384,384]{1,0:T(8,128)(2,1)S(1)} %maximum_select_fusion.10), channel_id=1, source_target_pairs={{0,2},{1,3},{2,0},{3,1},{4,6},{5,7},{6,4},{7,5},{8,10},{9,11},{10,... | collective-permute-start | bytes 884744 | tf_op jit(solution)/shard_map/ppermute | solution.py:576
  402.5 23.3 %copy-start.5 = (bf16[1,1,1024,768]{3,2,1,0:T(8,128)(2,1)S(1)}, bf16[1,1,1024,768]{3,2,1,0:T(8,128)(2,1)}, u32[]{:S(2)}) copy-start(bf16[1,1,1024,768]{3,2,1,0:T(8,128)(2,1)} %param.23) | copy-start | bytes 4718596
  402.5 23.2 %copy-start.8 = (f32[1024,768]{1,0:T(8,128)S(1)}, f32[1024,768]{1,0:T(8,128)}, u32[]{:S(2)}) copy-start(f32[1024,768]{1,0:T(8,128)} %get-tuple-element.97) | copy-start | bytes 9437188
  402.5 13.6 %collective-permute-start.29 = (bf16[192,768]{1,0:T(8,128)(2,1)S(1)}, bf16[192,768]{1,0:T(8,128)(2,1)S(1)}, u32[]{:S(2)}, u32[]{:S(2)}) collective-permute-start(bf16[192,768]{1,0:T(8,128)(2,1)S(1)} %maximum_select_fusion.11), channel_id=1, source_target_pairs={{0,2},{1,3},{2,0},{3,1},{4,6},{5,7},{6,4},{7,5},{8,10},{9,11},{10,... | collective-permute-start | bytes 884744 | tf_op jit(solution)/shard_map/ppermute | solution.py:576
  408.5 12.9 %collective-permute-start.20 = (bf16[512,384]{1,0:T(8,128)(2,1)S(1)}, bf16[512,384]{1,0:T(8,128)(2,1)S(1)}, u32[]{:S(2)}, u32[]{:S(2)}) collective-permute-start(bf16[512,384]{1,0:T(8,128)(2,1)S(1)} %maximum_select_fusion.9), channel_id=1, source_target_pairs={{0,2},{1,3},{2,0},{3,1},{4,6},{5,7},{6,4},{7,5},{8,10},{9,11},{10,... | collective-permute-start | bytes 1179656 | tf_op jit(solution)/shard_map/ppermute | solution.py:576
  408.8 21.3 %collective-permute-start.12 = (bf16[768,384]{1,0:T(8,128)(2,1)S(1)}, bf16[768,384]{1,0:T(8,128)(2,1)S(1)}, u32[]{:S(2)}, u32[]{:S(2)}) collective-permute-start(bf16[768,384]{1,0:T(8,128)(2,1)S(1)} %maximum_select_fusion.7), channel_id=1, source_target_pairs={{0,1},{1,0},{2,3},{3,2},{4,5},{5,4},{6,7},{7,6},{8,9},{9,8},{10,11... | collective-permute-start | bytes 1769480 | tf_op jit(solution)/shard_map/ppermute | solution.py:576
  416.4 12.1 %collective-permute-start.30 = (bf16[384,768]{1,0:T(8,128)(2,1)S(1)}, bf16[384,768]{1,0:T(8,128)(2,1)S(1)}, u32[]{:S(2)}, u32[]{:S(2)}) collective-permute-start(bf16[384,768]{1,0:T(8,128)(2,1)S(1)} %maximum_select_fusion.8), channel_id=1, source_target_pairs={{0,1},{1,0},{2,3},{3,2},{4,5},{5,4},{6,7},{7,6},{8,9},{9,8},{10,11... | collective-permute-start | bytes 1769480 | tf_op jit(solution)/shard_map/ppermute | solution.py:576
  421.7 8.8 %collective-permute-start.21 = (bf16[1024,384]{1,0:T(8,128)(2,1)S(1)}, bf16[1024,384]{1,0:T(8,128)(2,1)S(1)}, u32[]{:S(2)}, u32[]{:S(2)}) collective-permute-start(bf16[1024,384]{1,0:T(8,128)(2,1)S(1)} %maximum_select_fusion.6), channel_id=1, source_target_pairs={{0,1},{1,0},{2,3},{3,2},{4,5},{5,4},{6,7},{7,6},{8,9},{9,8},{10,11... | collective-permute-start | bytes 2359304 | tf_op jit(solution)/shard_map/ppermute | solution.py:576
